TPU v7x, 512 devices: a whole 4x4x16 slice. The times are simulated.
512 devices in a mesh: dp: 2 (over x_lo), ctx: 32 (over z, core), tp: 8 (over x_hi, y).
Axes of the slice: x: 4 (x_hi: 2, x_lo: 2; x = x_hi * 2 + x_lo), y: 4, z: 16, core: 2. Of those that a mesh axis runs over, the one named last changes fastest.
Arguments:
- query: bfloat16 [8192, 12288], P(('dp', 'ctx'), 'tp'), parts along dimension 0
- keys: bfloat16 [8192, 1024], P(('dp', 'ctx'), 'tp'), parts along dimension 0
- values: bfloat16 [8192, 1024], P(('dp', 'ctx'), 'tp'), parts along dimension 0, may hold values from -6 to 6
- doc_lengths: int32 [32], P('dp'), parts along dimension 0, may hold values from 1 to 2560, 4096 in all
- gain: bfloat16 [12288], P('tp'), may hold values from 0.5 to 1.5
Outputs:
- normed: bfloat16 [8192, 12288], P(('dp', 'ctx'), 'tp'), parts along dimension 0
There are 2 independent parts, one for each index of `dp`. A program takes and returns all parts, laid end to end along the dimension named above; an argument that names none is the same for every part. Nothing has to cross between parts.
Inputs may be any that keep to these rules, and one draw needn't show every extreme that they name: `doc_lengths`: the lengths sum to 4096; the longest is exactly 2560.
All inputs are finite; a program needn't handle non-finite values.
Results may differ from a plain program's by a relative error of at most 0.015.
Values may be sent and summed in bfloat16 or wider, within the bound.
No kernel may reach another device: no remote copies, remote signals or barrier semaphores. Data moves between devices by JAX's collectives and lax.ppermute only.
A program may use at most 64 MiB of HBM per device.

v0:
```python
import jax
import jax.numpy as jnp
from jax import lax
from jax.sharding import PartitionSpec as P

QUERY_HEADS = 96
HEAD_SIZE = 128


def body(query, keys, values, doc_lengths, gain):
    rows = query.shape[0]
    heads_local = query.shape[1] // HEAD_SIZE
    groups = keys.shape[1] // HEAD_SIZE
    query_group_ratio = heads_local // groups
    scale = HEAD_SIZE ** (-0.5)
    ends = jnp.cumsum(doc_lengths)

    def doc_index(positions):
        return jnp.sum((positions[:, None] >= ends[None, :]).astype(jnp.int32), axis=1)

    q_start = lax.axis_index("ctx") * rows
    q_pos = q_start + jnp.arange(rows, dtype=jnp.int32)
    q_doc = doc_index(q_pos)
    q_four = query.reshape(rows, groups, query_group_ratio, HEAD_SIZE)

    def attend(state, k_piece, v_piece, k_start):
        count = k_piece.shape[0]
        k_pos = k_start + jnp.arange(count, dtype=jnp.int32)
        k_doc = doc_index(k_pos)
        allowed = (
            (k_doc[None, :] == q_doc[:, None])
            & (k_pos[None, :] <= q_pos[:, None])
            & (k_pos[None, :] >= 0)
        )
        scores = (
            jnp.einsum(
                "sgrd,ngd->grsn",
                q_four,
                k_piece.reshape(count, groups, HEAD_SIZE),
                preferred_element_type=jnp.float32,
            )
            * scale
        )
        scores = jnp.where(allowed, scores, -1e30)
        top_old, total_old, acc_old = state
        top_new = jnp.maximum(top_old, jnp.max(scores, axis=-1))
        probs = jnp.where(allowed, jnp.exp(scores - top_new[..., None]), 0.0)
        correct = jnp.exp(top_old - top_new)
        total_new = total_old * correct + jnp.sum(probs, axis=-1)
        update = jnp.einsum(
            "grsn,ngd->grsd",
            probs.astype(jnp.bfloat16),
            v_piece.reshape(count, groups, HEAD_SIZE),
            preferred_element_type=jnp.float32,
        )
        return (top_new, total_new, acc_old * correct[..., None] + update)

    start_state = (
        jnp.full((groups, query_group_ratio, rows), -1e30, jnp.float32),
        jnp.zeros((groups, query_group_ratio, rows), jnp.float32),
        jnp.zeros((groups, query_group_ratio, rows, HEAD_SIZE), jnp.float32),
    )
    k_piece = lax.all_gather(keys, "ctx", axis=0, tiled=True)
    v_piece = lax.all_gather(values, "ctx", axis=0, tiled=True)
    count = k_piece.shape[0]
    block = 512

    def one_block(i, inner):
        k_block = lax.dynamic_slice_in_dim(k_piece, i * block, block, 0)
        v_block = lax.dynamic_slice_in_dim(v_piece, i * block, block, 0)
        return attend(inner, k_block, v_block, i * block)

    top, total, acc = lax.fori_loop(0, count // block, one_block, start_state)
    context = (
        jnp.transpose(acc / total[..., None], (2, 0, 1, 3))
        .reshape(rows, heads_local * HEAD_SIZE)
        .astype(jnp.bfloat16)
    )
    wide = context.astype(jnp.float32)
    squares_sum = lax.psum(jnp.sum(wide * wide, axis=1), "tp")
    power = squares_sum / (QUERY_HEADS * HEAD_SIZE)
    return (wide * gain.astype(jnp.float32)[None, :] / jnp.sqrt(power + 1e-06)[:, None]).astype(
        jnp.bfloat16
    )


def solution(mesh):
    return jax.shard_map(
        body,
        mesh=mesh,
        in_specs=(
            P(("dp", "ctx"), "tp"),
            P(("dp", "ctx"), "tp"),
            P(("dp", "ctx"), "tp"),
            P("dp"),
            P("tp"),
        ),
        out_specs=P(("dp", "ctx"), "tp"),
        check_vma=False,
    )
```

profile of v0, /device:TPU:1, one launch (start us, length us, event | category | flops | bytes accessed | tf_op | source)
XLA Modules:
  0.0 234.5 jit_solution(7426719118018077922)
XLA Ops:
  6.5 0.0 all-gather.3.cloned.1.call-start
  6.5 0.7 all-gather.3.cloned.1.call-update
  7.3 0.0 all-gather.5.cloned.1.call-start
  7.3 0.7 all-gather.5.cloned.1.call-update
  8.0 0.7 copy.16
  8.8 0.1 reduce.8
  8.9 1.2 copy.17
  10.1 0.9 copy.18
  11.1 0.7 convert_element_type.48
  11.8 0.1 convert_reduce_fusion.1
  11.9 74.0 %all-gather.3.cloned.1.call-done = bf16[4096,128]{1,0:T(8,128)(2,1)} async-done(((bf16[128,128]{1,0:T(8,128)(2,1)}), bf16[4096,128]{1,0:T(8,128)(2,1)}) %all-gather.3.cloned.1.call-update) | async-done | bytes 1048592 | tf_op jit(solution)/shard_map/all_gather | solution.py:63
  85.9 70.0 %all-gather.5.cloned.1.call-done = bf16[4096,128]{1,0:T(8,128)(2,1)} async-done(((bf16[128,128]{1,0:T(8,128)(2,1)}), bf16[4096,128]{1,0:T(8,128)(2,1)}) %all-gather.5.cloned.1.call-update) | async-done | bytes 1048592 | tf_op jit(solution)/shard_map/all_gather | solution.py:64
  155.8 48.6 %while.18 = (s32[]{:T(128)}, f32[1,12,128]{2,1,0:T(8,128)S(1)}, f32[1,12,128]{2,1,0:T(8,128)S(1)}, f32[1,12,128,128]{3,2,1,0:T(8,128)}, s32[16]{0:T(128)S(1)}, /...) while((s32[]{:T(128)}, f32[1,12,128]{2,1,0:T(8,128)S(1)}, ...), condition=%wide.region_6.7_spmd.clone, body=%wide.region_2.6_spmd.clone.sunk | while | flops 413763712 | bytes 12038931 | solution.py:73
  155.9 0.1 convert_reduce_fusion.3
  156.0 0.3 and_and_fusion.2
  156.2 1.7 fusion.39
  157.9 2.9 %fusion.42 = f32[1,12,128,128]{3,2,1,0:T(8,128)} fusion(f32[512,128,12]{1,0,2:T(8,128)S(1)} %get-tuple-element.326, f32[12,128]{1,0:T(8,128)S(1)} %bitcast.84, pred[128,512]{0,1:T(8,128)(4,1)S(1)} %and_and_fusion.2, f32[1,12,128,128]{3,2,1,0:T(8,128)} %get-tuple-element.345, f32[12,128]{1,0:T(8,128)S(1)} %get-tuple-element.327, pred[]{:T(512)S(6)} %compare.3, ...), kind=kOutput, calls=%fused_computation.10.clone.1 | convolution fusion | flops 205848576 | bytes 4927493 | tf_op jit(solution)/shard_map/while/body/eval_jaxpr/grsn,ngd->grsd/dot_general | solution.py:50
  160.8 0.8 fusion.41
  161.7 0.1 convert_reduce_fusion.3
  161.8 0.3 and_and_fusion.2
  162.0 1.7 fusion.39
  163.7 3.2 %fusion.42 = f32[1,12,128,128]{3,2,1,0:T(8,128)} fusion(f32[512,128,12]{1,0,2:T(8,128)S(1)} %get-tuple-element.326, f32[12,128]{1,0:T(8,128)S(1)} %bitcast.84, pred[128,512]{0,1:T(8,128)(4,1)S(1)} %and_and_fusion.2, f32[1,12,128,128]{3,2,1,0:T(8,128)} %get-tuple-element.345, f32[12,128]{1,0:T(8,128)S(1)} %get-tuple-element.327, pred[]{:T(512)S(6)} %compare.3, ...), kind=kOutput, calls=%fused_computation.10.clone.1 | convolution fusion | flops 205848576 | bytes 4927493 | tf_op jit(solution)/shard_map/while/body/eval_jaxpr/grsn,ngd->grsd/dot_general | solution.py:50
  166.9 0.8 fusion.41
  167.8 0.1 convert_reduce_fusion.3
  167.9 0.3 and_and_fusion.2
  168.2 1.7 fusion.39
  169.8 3.2 %fusion.42 = f32[1,12,128,128]{3,2,1,0:T(8,128)} fusion(f32[512,128,12]{1,0,2:T(8,128)S(1)} %get-tuple-element.326, f32[12,128]{1,0:T(8,128)S(1)} %bitcast.84, pred[128,512]{0,1:T(8,128)(4,1)S(1)} %and_and_fusion.2, f32[1,12,128,128]{3,2,1,0:T(8,128)} %get-tuple-element.345, f32[12,128]{1,0:T(8,128)S(1)} %get-tuple-element.327, pred[]{:T(512)S(6)} %compare.3, ...), kind=kOutput, calls=%fused_computation.10.clone.1 | convolution fusion | flops 205848576 | bytes 4927493 | tf_op jit(solution)/shard_map/while/body/eval_jaxpr/grsn,ngd->grsd/dot_general | solution.py:50
  173.1 0.8 fusion.41
  173.9 0.1 convert_reduce_fusion.3
  174.0 0.3 and_and_fusion.2
  174.3 1.7 fusion.39
  176.0 3.2 %fusion.42 = f32[1,12,128,128]{3,2,1,0:T(8,128)} fusion(f32[512,128,12]{1,0,2:T(8,128)S(1)} %get-tuple-element.326, f32[12,128]{1,0:T(8,128)S(1)} %bitcast.84, pred[128,512]{0,1:T(8,128)(4,1)S(1)} %and_and_fusion.2, f32[1,12,128,128]{3,2,1,0:T(8,128)} %get-tuple-element.345, f32[12,128]{1,0:T(8,128)S(1)} %get-tuple-element.327, pred[]{:T(512)S(6)} %compare.3, ...), kind=kOutput, calls=%fused_computation.10.clone.1 | convolution fusion | flops 205848576 | bytes 4927493 | tf_op jit(solution)/shard_map/while/body/eval_jaxpr/grsn,ngd->grsd/dot_general | solution.py:50
  179.2 0.8 fusion.41
  180.0 0.1 convert_reduce_fusion.3
  180.1 0.3 and_and_fusion.2
  180.4 1.7 fusion.39
  182.1 3.2 %fusion.42 = f32[1,12,128,128]{3,2,1,0:T(8,128)} fusion(f32[512,128,12]{1,0,2:T(8,128)S(1)} %get-tuple-element.326, f32[12,128]{1,0:T(8,128)S(1)} %bitcast.84, pred[128,512]{0,1:T(8,128)(4,1)S(1)} %and_and_fusion.2, f32[1,12,128,128]{3,2,1,0:T(8,128)} %get-tuple-element.345, f32[12,128]{1,0:T(8,128)S(1)} %get-tuple-element.327, pred[]{:T(512)S(6)} %compare.3, ...), kind=kOutput, calls=%fused_computation.10.clone.1 | convolution fusion | flops 205848576 | bytes 4927493 | tf_op jit(solution)/shard_map/while/body/eval_jaxpr/grsn,ngd->grsd/dot_general | solution.py:50
  185.3 0.8 fusion.41
  186.1 0.1 convert_reduce_fusion.3
  186.2 0.3 and_and_fusion.2
  186.5 1.7 fusion.39
  188.2 3.2 %fusion.42 = f32[1,12,128,128]{3,2,1,0:T(8,128)} fusion(f32[512,128,12]{1,0,2:T(8,128)S(1)} %get-tuple-element.326, f32[12,128]{1,0:T(8,128)S(1)} %bitcast.84, pred[128,512]{0,1:T(8,128)(4,1)S(1)} %and_and_fusion.2, f32[1,12,128,128]{3,2,1,0:T(8,128)} %get-tuple-element.345, f32[12,128]{1,0:T(8,128)S(1)} %get-tuple-element.327, pred[]{:T(512)S(6)} %compare.3, ...), kind=kOutput, calls=%fused_computation.10.clone.1 | convolution fusion | flops 205848576 | bytes 4927493 | tf_op jit(solution)/shard_map/while/body/eval_jaxpr/grsn,ngd->grsd/dot_general | solution.py:50
  191.4 0.8 fusion.41
  192.2 0.1 convert_reduce_fusion.3
  192.3 0.3 and_and_fusion.2
  192.6 1.7 fusion.39
  194.3 3.2 %fusion.42 = f32[1,12,128,128]{3,2,1,0:T(8,128)} fusion(f32[512,128,12]{1,0,2:T(8,128)S(1)} %get-tuple-element.326, f32[12,128]{1,0:T(8,128)S(1)} %bitcast.84, pred[128,512]{0,1:T(8,128)(4,1)S(1)} %and_and_fusion.2, f32[1,12,128,128]{3,2,1,0:T(8,128)} %get-tuple-element.345, f32[12,128]{1,0:T(8,128)S(1)} %get-tuple-element.327, pred[]{:T(512)S(6)} %compare.3, ...), kind=kOutput, calls=%fused_computation.10.clone.1 | convolution fusion | flops 205848576 | bytes 4927493 | tf_op jit(solution)/shard_map/while/body/eval_jaxpr/grsn,ngd->grsd/dot_general | solution.py:50
  197.5 0.8 fusion.41
  198.3 0.1 convert_reduce_fusion.3
  198.4 0.3 and_and_fusion.2
  198.7 1.7 fusion.39
  200.4 3.2 %fusion.42 = f32[1,12,128,128]{3,2,1,0:T(8,128)} fusion(f32[512,128,12]{1,0,2:T(8,128)S(1)} %get-tuple-element.326, f32[12,128]{1,0:T(8,128)S(1)} %bitcast.84, pred[128,512]{0,1:T(8,128)(4,1)S(1)} %and_and_fusion.2, f32[1,12,128,128]{3,2,1,0:T(8,128)} %get-tuple-element.345, f32[12,128]{1,0:T(8,128)S(1)} %get-tuple-element.327, pred[]{:T(512)S(6)} %compare.3, ...), kind=kOutput, calls=%fused_computation.10.clone.1 | convolution fusion | flops 205848576 | bytes 4927493 | tf_op jit(solution)/shard_map/while/body/eval_jaxpr/grsn,ngd->grsd/dot_general | solution.py:50
  203.6 0.8 fusion.41
  204.4 1.4 copy.19
  205.8 0.2 multiply_reduce_fusion
  206.0 20.3 %psum.7 = f32[128]{0:T(128)S(1)} all-reduce(f32[128]{0:T(128)S(1)} %get-tuple-element.255), channel_id=1, replica_groups=mesh['dp'=2,'ctx'=32,'tp'=8] {'tp'}, use_global_device_ids=true, to_apply=%region_8.9 | all-reduce | flops 128 | bytes 1024 | tf_op jit(solution)/shard_map/psum | solution.py:80
  226.4 0.3 fusion.28
  226.7 0.9 copy.20
  (54 shorter events, 0.4 us)
Async XLA Ops:
  6.5 79.3 %all-gather.3.cloned.1.call-start = ((), (), s32[]{:S(2)}) async-start(), calls=%async_computation | async-start | bytes 1081344 | tf_op jit(solution)/shard_map/all_gather | solution.py:63
  7.3 148.6 %all-gather.5.cloned.1.call-start = ((), (), s32[]{:S(2)}) async-start(), calls=%async_computation.1 | async-start | bytes 1081344 | tf_op jit(solution)/shard_map/all_gather | solution.py:64
Sparse Core Ops, SparseCore 0:
  9.5 76.3 all-gather.2
  88.0 67.8 all-gather.4
where the time goes:
time: 237 us; the launch traced here: 234 us
  waiting for transfers between devices  145 us (61%)
  matrix products  38.7 us (16%)
  blocking collectives  20.3 us (9%)
  between operations  13.5 us (6%)
  other arithmetic  10.7 us (5%)
  local copies, waits for them, and re-layouts  5.24 us (2%)
    all_gather x1, waiting for transfers between devices, body(): k_piece = lax.all_gather(keys, 'ctx', axis=0, tiled=True)  74 us
    all_gather x1, waiting for transfers between devices, body(): v_piece = lax.all_gather(values, 'ctx', axis=0, tiled=True)  70 us
    dot_general x8, matrix products, attend(): jnp.einsum('grsn,ngd->grsd', probs.astype(jnp.bfloat16), v_piece.reshape(...  25.4 us
    psum x1, blocking collectives, body(): squares_sum = lax.psum(jnp.sum(wide * wide, axis=1), 'tp')  20.3 us
    dot_general x8, matrix products, attend(): jnp.einsum('sgrd,ngd->grsn', q_four, k_piece.reshape(count, groups, HEAD_...  13.3 us
    reduce_sum x8, other arithmetic, attend(): total_new = total_old * correct + jnp.sum(probs, axis=-1)  6.1 us
  transfers between devices with their start and end apart: 2, of which 2 were waited for; matrix products, arithmetic and copies ran while one was open for 2% of the time, Pallas kernels for 0%

commit v1 on v0

v1 whole, which is shorter than its diff:
```python
import functools

import jax
import jax.numpy as jnp
from jax import lax
from jax.experimental import pallas as pl
from jax.experimental.pallas import tpu as pltpu
from jax.sharding import Mesh, PartitionSpec as P

QUERY_HEADS = 96
HEAD_SIZE = 128
ROWS = 128
MASKED = -1e30
EXP2_SCALE = HEAD_SIZE ** (-0.5) * 1.4426950408889634


def doc_starts(lengths_ref, q_pos):
    start = jnp.zeros_like(q_pos)
    end = jnp.int32(0)
    for i in range(lengths_ref.shape[0]):
        end = end + lengths_ref[i]
        start = jnp.maximum(start, jnp.where(q_pos >= end, end, 0))
    return start


def attend(step, distances, head_block, first, last, *refs):
    refs = list(refs)
    where_ref, lengths_ref, q_ref = refs[:3]
    pieces = refs[3 : 3 + len(distances)]
    rest = refs[3 + len(distances) :]
    if not first:
        m_in, l_in, acc_in = rest[:3]
        rest = rest[3:]
    if last:
        ctx_ref, squares_ref, bias_ref, k_ref, v_ref = rest
    else:
        m_out, l_out, acc_out, bias_ref, k_ref, v_ref = rest
    chip, core = where_ref[0], where_ref[1]
    q_pos = chip * (2 * ROWS) + core * ROWS + lax.broadcasted_iota(jnp.int32, (ROWS, ROWS), 0)
    start = doc_starts(lengths_ref, q_pos)
    lane = lax.broadcasted_iota(jnp.int32, (ROWS, ROWS), 1)
    at = 0
    for piece, (mine, back) in zip(pieces, distances):
        for j, d in enumerate(back):
            rows = pl.ds(at * ROWS, ROWS)
            k_ref[rows, :] = piece[j * ROWS : (j + 1) * ROWS, :HEAD_SIZE]
            v_ref[rows, :HEAD_SIZE] = piece[j * ROWS : (j + 1) * ROWS, HEAD_SIZE:]
            holder = core if mine else 1 - core
            k_pos = (chip - d) * (2 * ROWS) + holder * ROWS + lane
            allowed = (k_pos >= start) & (k_pos <= q_pos)
            bias_ref[:, rows] = jnp.where(allowed, 0.0, MASKED)
            at += 1
    v_ref[:, HEAD_SIZE:] = jnp.ones_like(v_ref[:, HEAD_SIZE:])
    squares = jnp.zeros((ROWS, HEAD_SIZE), jnp.float32)
    heads = q_ref.shape[1] // HEAD_SIZE
    for h0 in range(0, heads, head_block):
        q = jnp.concatenate(
            [q_ref[:, h * HEAD_SIZE : (h + 1) * HEAD_SIZE] for h in range(h0, h0 + head_block)], axis=0
        )
        s = lax.dot_general(q, k_ref[...], (((1,), (1,)), ((), ())), preferred_element_type=jnp.float32)
        s = s.reshape(head_block, ROWS, -1) + bias_ref[...][None]
        top = jnp.max(s, axis=-1, keepdims=True)
        if not first:
            m_old = m_in[h0 : h0 + head_block]
            top = jnp.maximum(top, m_old[:, :, :1])
        p = jnp.exp2((s - top) * EXP2_SCALE).astype(jnp.bfloat16)
        out = lax.dot_general(
            p.reshape(head_block * ROWS, -1), v_ref[...], (((1,), (0,)), ((), ())), preferred_element_type=jnp.float32
        ).reshape(head_block, ROWS, 2 * HEAD_SIZE)
        acc, total = out[:, :, :HEAD_SIZE], out[:, :, HEAD_SIZE:]
        if not first:
            correct = jnp.exp2((m_old - top) * EXP2_SCALE)
            acc = acc + acc_in[h0 : h0 + head_block] * correct
            total = total + l_in[h0 : h0 + head_block] * correct
        if last:
            context = (acc / total).astype(jnp.bfloat16)
            for h in range(head_block):
                ctx_ref[:, (h0 + h) * HEAD_SIZE : (h0 + h + 1) * HEAD_SIZE] = context[h]
                wide = context[h].astype(jnp.float32)
                squares = squares + wide * wide
        else:
            m_out[h0 : h0 + head_block] = jnp.broadcast_to(top, acc.shape)
            l_out[h0 : h0 + head_block] = total
            acc_out[h0 : h0 + head_block] = acc
    if last:
        summed = jnp.sum(squares.T, axis=0, keepdims=True)
        squares_ref[...] = jnp.broadcast_to(summed, squares_ref.shape)


def attention(where, lengths, query, pieces, distances, state, last, head_block):
    heads = query.shape[1] // HEAD_SIZE
    keys = sum(len(back) for _, back in distances) * ROWS
    vmem = pl.BlockSpec(memory_space=pltpu.VMEM)
    smem = pl.BlockSpec(memory_space=pltpu.SMEM)
    state = [] if state is None else list(state)
    if last:
        out_shape = (
            jax.ShapeDtypeStruct(query.shape, jnp.bfloat16),
            jax.ShapeDtypeStruct((8, ROWS), jnp.float32),
        )
    else:
        out_shape = (jax.ShapeDtypeStruct((heads, ROWS, HEAD_SIZE), jnp.float32),) * 3
    work = heads * ROWS * keys
    return pl.pallas_call(
        functools.partial(attend, 0, distances, head_block, not state, last),
        out_shape=out_shape,
        in_specs=[smem, smem] + [vmem] * (1 + len(pieces) + len(state)),
        out_specs=tuple([vmem] * len(out_shape)),
        scratch_shapes=[
            pltpu.VMEM((ROWS, keys), jnp.float32),
            pltpu.VMEM((keys, HEAD_SIZE), jnp.bfloat16),
            pltpu.VMEM((keys, 2 * HEAD_SIZE), jnp.bfloat16),
        ],
        compiler_params=pltpu.CompilerParams(vmem_limit_bytes=40 * 1024 * 1024),
        cost_estimate=pl.CostEstimate(flops=4 * work * HEAD_SIZE, bytes_accessed=4 << 20, transcendentals=work),
        name="attention_last" if last else "attention_first",
    )(where, lengths, query, *pieces, *state)


def scale_rows(ctx_ref, squares_ref, gain_ref, out_ref):
    power = jnp.sum(squares_ref[...], axis=0)[:1] / (QUERY_HEADS * HEAD_SIZE)
    factor = lax.rsqrt(jnp.broadcast_to(power, (ROWS, ROWS)).T + 1e-06)
    for h in range(ctx_ref.shape[1] // HEAD_SIZE):
        lanes = slice(h * HEAD_SIZE, (h + 1) * HEAD_SIZE)
        gain = gain_ref[:, lanes].astype(jnp.float32)
        out_ref[:, lanes] = (ctx_ref[:, lanes].astype(jnp.float32) * gain * factor).astype(jnp.bfloat16)


def body(query, keys, values, doc_lengths, gain):
    chips = lax.axis_size("chip")

    def shift(x, by):
        return lax.ppermute(x, "chip", [(i, (i + by) % chips) for i in range(chips)])

    def sibling(x):
        return lax.ppermute(x, "core", [(0, 1), (1, 0)])

    where = jnp.stack([lax.axis_index("chip"), lax.axis_index("core")]).astype(jnp.int32)
    own = jnp.concatenate([keys, values], axis=1)
    r1 = shift(own, 1)
    r2 = shift(own, 2)
    r10 = shift(own, -6)
    near = jnp.concatenate([own, r1, r2], axis=0)
    r9 = shift(r10, -1)
    r8 = shift(r10, -2)
    r7 = shift(r10, -3)
    r6 = shift(r2, 4)
    r345 = shift(near, 3)
    other_first = sibling(jnp.concatenate([near, r10], axis=0))
    state = attention(
        where, doc_lengths, query,
        (near, r10, other_first),
        ((True, (0, 1, 2)), (True, (10,)), (False, (0, 1, 2, 10))),
        None, False, 3,
    )
    other_last = sibling(jnp.concatenate([r345, r6, r7, r8, r9], axis=0))
    context, squares = attention(
        where, doc_lengths, query,
        (r345, r6, r7, r8, r9, other_last),
        ((True, (3, 4, 5)), (True, (6,)), (True, (7,)), (True, (8,)), (True, (9,)), (False, (3, 4, 5, 6, 7, 8, 9))),
        state, True, 2,
    )
    all_squares = lax.all_to_all(jnp.broadcast_to(squares, (8,) + squares.shape), "tp", 0, 0)
    return pl.pallas_call(
        scale_rows,
        out_shape=jax.ShapeDtypeStruct(query.shape, jnp.bfloat16),
        compiler_params=pltpu.CompilerParams(vmem_limit_bytes=16 * 1024 * 1024),
    )(context, all_squares, gain.reshape(1, -1))


def solution(mesh):
    sizes = mesh.shape
    fine = Mesh(
        mesh.devices.reshape(sizes["dp"], sizes["ctx"] // 2, 2, sizes["tp"]), ("dp", "chip", "core", "tp")
    )
    tokens = ("dp", "chip", "core")
    return jax.shard_map(
        body,
        mesh=fine,
        in_specs=(P(tokens, "tp"), P(tokens, "tp"), P(tokens, "tp"), P("dp"), P("tp")),
        out_specs=P(tokens, "tp"),
        check_vma=False,
    )
```

time: 237 us -> 84.8 us (0.36)
  waiting for transfers between devices: 145 us -> 19 us
  starting transfers between devices: 0.04 us -> 54.2 us
  matrix products: 38.7 us -> 0 us
  blocking collectives: 20.3 us -> 0 us
  between operations: 13.5 us -> 0.22 us
  other arithmetic: 10.7 us -> 0.11 us
  Pallas kernels: 0 us -> 9.24 us
  local copies, waits for them, and re-layouts: 5.24 us -> 1.48 us
    all_gather x2 -> x0, waiting for transfers between devices: 144 us -> none  [the longest x1 74 us: body(): k_piece = lax.all_gather(keys, 'ctx', axis=0, tiled=True)]
    ppermute x0 -> x10, starting transfers between devices: none -> 47.5 us  [the longest x8 41.4 us: shift(): lax.ppermute(x, 'chip', [(i, (i + by) % chips) for i in range(chips)])]
    dot_general x16 -> x0, matrix products: 38.7 us -> none  [the longest x8 25.4 us: attend(): jnp.einsum('grsn,ngd->grsd', probs.astype(jnp.bfloat16), v_piece.reshape(...]
    psum x1 -> x0, blocking collectives: 20.3 us -> none  [body(): squares_sum = lax.psum(jnp.sum(wide * wide, axis=1), 'tp')]
    ppermute x0 -> x10, waiting for transfers between devices: none -> 12.4 us  [the longest x8 11 us: shift(): lax.ppermute(x, 'chip', [(i, (i + by) % chips) for i in range(chips)])]
    pallas_call x0 -> x3, Pallas kernels: none -> 9.24 us  [the longest x2 8.34 us: attention(): pl.pallas_call(functools.partial(attend, 0, distances, head_block, not st...]
    reduce_sum x18 -> x0, other arithmetic: 7.13 us -> none  [the longest x8 6.1 us: attend(): total_new = total_old * correct + jnp.sum(probs, axis=-1)]
    all_to_all x0 -> x1, starting transfers between devices: none -> 6.78 us  [body(): lax.all_to_all(jnp.broadcast_to(squares, (8,) + squares.shape), 'tp', 0, 0)]
  transfers between devices with their start and end apart: 2 -> 11, of which waited for: 2 -> 6; matrix products, arithmetic and copies ran while one was open for 2% -> 0% of each run, Pallas kernels for 0% -> 4%
where the time goes in v1:
time: 84.8 us; the launch traced here: 84.3 us
  starting transfers between devices  54.2 us (64%)
  waiting for transfers between devices  19 us (22%)
  Pallas kernels  9.24 us (11%)
  local copies, waits for them, and re-layouts  1.48 us (2%)
    ppermute x8, starting transfers between devices, shift(): lax.ppermute(x, 'chip', [(i, (i + by) % chips) for i in range(chips)])  41.4 us
    ppermute x8, waiting for transfers between devices, shift(): lax.ppermute(x, 'chip', [(i, (i + by) % chips) for i in range(chips)])  11 us
    pallas_call x2, Pallas kernels, attention(): pl.pallas_call(functools.partial(attend, 0, distances, head_block, not st...  8.34 us
    all_to_all x1, starting transfers between devices, body(): lax.all_to_all(jnp.broadcast_to(squares, (8,) + squares.shape), 'tp', 0, 0)  6.78 us
    all_to_all x1, waiting for transfers between devices, body(): lax.all_to_all(jnp.broadcast_to(squares, (8,) + squares.shape), 'tp', 0, 0)  6.59 us
    ppermute x2, starting transfers between devices, sibling(): return lax.ppermute(x, 'core', [(0, 1), (1, 0)])  6.02 us
  transfers between devices with their start and end apart: 11, of which 6 were waited for; matrix products, arithmetic and copies ran while one was open for 0% of the time, Pallas kernels for 4%

profile of v1, /device:TPU:1, one launch (start us, length us, event | category | flops | bytes accessed | tf_op | source)
XLA Modules:
  0.0 84.3 jit_solution(8572064277512720405)
XLA Ops:
  0.0 0.0 copy-start.2
  0.0 0.8 constant_dynamic-update-slice_fusion.1
  0.8 0.0 copy-done.2
  0.8 5.7 %collective-permute-start.1 = (bf16[128,256]{1,0:T(8,128)(2,1)S(1)}, bf16[128,256]{1,0:T(8,128)(2,1)S(1)}, u32[]{:S(2)}, u32[]{:S(2)}) collective-permute-start(bf16[128,256]{1,0:T(8,128)(2,1)S(1)} %constant_dynamic-update-slice_fusion), channel_id=1, source_target_pairs={{0,32},{16,48},{32,64},{48,80},{64,96},{80,112},{96,128},{112,144}... | collective-permute-start | bytes 196616 | tf_op jit(solution)/shard_map/ppermute | solution.py:133
  6.5 3.5 %collective-permute-start = (bf16[128,256]{1,0:T(8,128)(2,1)S(1)}, bf16[128,256]{1,0:T(8,128)(2,1)S(1)}, u32[]{:S(2)}, u32[]{:S(2)}) collective-permute-start(bf16[128,256]{1,0:T(8,128)(2,1)S(1)} %constant_dynamic-update-slice_fusion), channel_id=1, source_target_pairs={{0,16},{16,32},{32,48},{48,64},{64,80},{80,96},{96,112},{112,128},... | collective-permute-start | bytes 196616 | tf_op jit(solution)/shard_map/ppermute | solution.py:133
  10.1 4.9 %collective-permute-done.1 = bf16[128,256]{1,0:T(8,128)(2,1)S(1)} collective-permute-done((bf16[128,256]{1,0:T(8,128)(2,1)S(1)}, bf16[128,256]{1,0:T(8,128)(2,1)S(1)}, u32[]{:S(2)}, u32[]{:S(2)}) %collective-permute-start.1) | collective-permute-done | bytes 65568 | tf_op jit(solution)/shard_map/ppermute | solution.py:133
  14.9 2.7 %collective-permute-done = bf16[128,256]{1,0:T(8,128)(2,1)S(1)} collective-permute-done((bf16[128,256]{1,0:T(8,128)(2,1)S(1)}, bf16[128,256]{1,0:T(8,128)(2,1)S(1)}, u32[]{:S(2)}, u32[]{:S(2)}) %collective-permute-start) | collective-permute-done | bytes 65568 | tf_op jit(solution)/shard_map/ppermute | solution.py:133
  17.7 1.9 %collective-permute-start.2 = (bf16[384,256]{1,0:T(8,128)(2,1)S(1)}, bf16[384,256]{1,0:T(8,128)(2,1)S(1)}, u32[]{:S(2)}, u32[]{:S(2)}) collective-permute-start(bf16[384,256]{1,0:T(8,128)(2,1)S(1)} %pad_maximum_fusion.1.refs_3_), channel_id=1, source_target_pairs={{0,48},{16,64},{32,80},{48,96},{64,112},{80,128},{96,144},{112,160... | collective-permute-start | bytes 589832 | tf_op jit(solution)/shard_map/ppermute | solution.py:133
  19.6 9.0 %collective-permute-start.4 = (bf16[128,256]{1,0:T(8,128)(2,1)S(1)}, bf16[128,256]{1,0:T(8,128)(2,1)S(1)}, u32[]{:S(2)}, u32[]{:S(2)}) collective-permute-start(bf16[128,256]{1,0:T(8,128)(2,1)S(1)} %constant_dynamic-update-slice_fusion), channel_id=1, source_target_pairs={{0,160},{16,176},{32,192},{48,208},{64,224},{80,240},{96,0},{112,1... | collective-permute-start | bytes 196616 | tf_op jit(solution)/shard_map/ppermute | solution.py:133
  28.6 3.0 %collective-permute-start.3 = (bf16[128,256]{1,0:T(8,128)(2,1)S(1)}, bf16[128,256]{1,0:T(8,128)(2,1)S(1)}, u32[]{:S(2)}, u32[]{:S(2)}) collective-permute-start(bf16[128,256]{1,0:T(8,128)(2,1)S(1)} %collective-permute-done.1), channel_id=1, source_target_pairs={{0,64},{16,80},{32,96},{48,112},{64,128},{80,144},{96,160},{112,17... | collective-permute-start | bytes 196616 | tf_op jit(solution)/shard_map/ppermute | solution.py:133
  31.6 0.4 collective-permute-done.4.refs_4_
  32.0 12.4 %collective-permute-start.5 = (bf16[128,256]{1,0:T(8,128)(2,1)S(1)}, bf16[128,256]{1,0:T(8,128)(2,1)S(1)}, u32[]{:S(2)}, u32[]{:S(2)}) collective-permute-start(bf16[128,256]{1,0:T(8,128)(2,1)S(1)} %collective-permute-done.4.refs_4_), channel_id=1, source_target_pairs={{0,208},{16,224},{32,240},{48,0},{64,16},{80,32},{96,48},{112,64},... | collective-permute-start | bytes 196616 | tf_op jit(solution)/shard_map/ppermute | solution.py:133
  44.4 4.0 %collective-permute-start.6 = (bf16[128,256]{1,0:T(8,128)(2,1)S(1)}, bf16[128,256]{1,0:T(8,128)(2,1)S(1)}, u32[]{:S(2)}, u32[]{:S(2)}) collective-permute-start(bf16[128,256]{1,0:T(8,128)(2,1)S(1)} %collective-permute-done.4.refs_4_), channel_id=1, source_target_pairs={{0,224},{16,240},{32,0},{48,16},{64,32},{80,48},{96,64},{112,80},{... | collective-permute-start | bytes 196616 | tf_op jit(solution)/shard_map/ppermute | solution.py:133
  48.4 1.9 %collective-permute-start.7 = (bf16[128,256]{1,0:T(8,128)(2,1)S(1)}, bf16[128,256]{1,0:T(8,128)(2,1)S(1)}, u32[]{:S(2)}, u32[]{:S(2)}) collective-permute-start(bf16[128,256]{1,0:T(8,128)(2,1)S(1)} %collective-permute-done.4.refs_4_), channel_id=1, source_target_pairs={{0,240},{16,0},{32,16},{48,32},{64,48},{80,64},{96,80},{112,96},{1... | collective-permute-start | bytes 196616 | tf_op jit(solution)/shard_map/ppermute | solution.py:133
  50.3 0.0 collective-permute-done.2.refs_3_
  50.3 0.0 collective-permute-done.3.refs_4_
  50.4 0.0 collective-permute-done.5.refs_5_
  50.4 0.0 copy-start
  50.4 0.0 collective-permute-done.6.refs_6_
  50.4 3.0 %collective-permute-done.7.refs_7_ = bf16[128,256]{1,0:T(8,128)(2,1)S(1)} collective-permute-done((bf16[128,256]{1,0:T(8,128)(2,1)S(1)}, bf16[128,256]{1,0:T(8,128)(2,1)S(1)}, u32[]{:S(2)}, u32[]{:S(2)}) %collective-permute-start.7) | collective-permute-done | bytes 65568 | tf_op jit(solution)/shard_map/ppermute | solution.py:133
  53.4 4.1 %collective-permute-start.8 = (bf16[896,256]{1,0:T(8,128)(2,1)S(1)}, bf16[896,256]{1,0:T(8,128)(2,1)S(1)}, u32[]{:S(2)}, u32[]{:S(2)}) collective-permute-start(bf16[896,256]{1,0:T(8,128)(2,1)S(1)} %constant_dynamic-update-slice_fusion.2), channel_id=1, source_target_pairs={{0,8},{8,0},{1,9},{9,1},{2,10},{10,2},{3,11},{11,3},{4,12},{12,4},... | collective-permute-start | bytes 1376264 | tf_op jit(solution)/shard_map/ppermute | solution.py:136
  57.5 1.9 %collective-permute-start.9 = (bf16[512,256]{1,0:T(8,128)(2,1)S(1)}, bf16[512,256]{1,0:T(8,128)(2,1)S(1)}, u32[]{:S(2)}, u32[]{:S(2)}) collective-permute-start(bf16[512,256]{1,0:T(8,128)(2,1)S(1)} %pad_maximum_fusion), channel_id=1, source_target_pairs={{0,8},{8,0},{1,9},{9,1},{2,10},{10,2},{3,11},{11,3},{4,12},{12,4},... | collective-permute-start | bytes 786440 | tf_op jit(solution)/shard_map/ppermute | solution.py:136
  59.5 0.0 copy-start.1
  59.5 0.1 pad_add_fusion.refs_0_
  59.6 1.4 %collective-permute-done.9.refs_5_ = bf16[512,256]{1,0:T(8,128)(2,1)S(1)} collective-permute-done((bf16[512,256]{1,0:T(8,128)(2,1)S(1)}, bf16[512,256]{1,0:T(8,128)(2,1)S(1)}, u32[]{:S(2)}, u32[]{:S(2)}) %collective-permute-start.9) | collective-permute-done | bytes 262176 | tf_op jit(solution)/shard_map/ppermute | solution.py:136
  61.0 0.0 copy-done
  61.0 0.0 copy-done.1
  61.0 3.2 %attention_first.1 = (f32[12,128,128]{2,1,0:T(8,128)S(1)}, f32[12,128,128]{2,1,0:T(8,128)S(1)}, f32[12,128,128]{2,1,0:T(8,128)S(1)}) custom-call(s32[2]{0:T(128)S(1)} %pad_add_fusion.refs_0_, s32[16]{0:T(128)S(1)} %copy-done.1, bf16[128,1536]{1,0:T(8,128)(2,1)S(1)} %copy-done, bf16[384,256]{1,0:T(8,128)(2,1)S(1)} %pad_maximum_fusion.1.refs_3_, ...), custom_call_target="tpu_custom_call" | custom-call | flops 805306368 | bytes 4194304 | tf_op jit(solution)/shard_map/attention_first/pallas_call | solution.py:104
  64.2 0.0 collective-permute-done.8.refs_8_
  64.2 5.1 %attention_last.1 = (bf16[128,1536]{1,0:T(8,128)(2,1)S(1)}, f32[8,128]{1,0:T(8,128)S(1)}) custom-call(s32[2]{0:T(128)S(1)} %pad_add_fusion.refs_0_, s32[16]{0:T(128)S(1)} %copy-done.1, bf16[128,1536]{1,0:T(8,128)(2,1)S(1)} %copy-done, bf16[384,256]{1,0:T(8,128)(2,1)S(1)} %collective-permute-done.2.refs_3_, ...), custom_call_target="tpu_custom_call" | custom-call | flops 1409286144 | bytes 4194304 | tf_op jit(solution)/shard_map/attention_last/pallas_call | solution.py:104
  69.3 0.6 broadcast_in_dim.3
  70.0 0.0 copy-start.3
  70.0 6.8 %all-to-all-start = ((f32[8,8,128]{2,1,0:T(8,128)}), f32[8,8,128]{2,1,0:T(8,128)S(1)}, u32[]{:S(2)}, u32[]{:S(2)}) async-start(f32[8,8,128]{2,1,0:T(8,128)} %broadcast_in_dim.3), calls=%async_computation | async-start | bytes 65536 | tf_op jit(solution)/shard_map/all_to_all | solution.py:163
  76.7 0.0 copy-done.3
  76.8 6.6 %all-to-all-done.squares_ref = f32[8,8,128]{2,1,0:T(8,128)S(1)} async-done(((f32[8,8,128]{2,1,0:T(8,128)}), f32[8,8,128]{2,1,0:T(8,128)S(1)}, u32[]{:S(2)}, u32[]{:S(2)}) %all-to-all-start) | async-done | bytes 32800 | tf_op jit(solution)/shard_map/all_to_all | solution.py:163
  83.4 0.9 %shard_map.55 = bf16[128,1536]{1,0:T(8,128)(2,1)} custom-call(bf16[128,1536]{1,0:T(8,128)(2,1)S(1)} %get-tuple-element.13.ctx_ref, f32[8,8,128]{2,1,0:T(8,128)S(1)} %all-to-all-done.squares_ref, bf16[1,1536]{1,0:T(2,128)(2,1)S(1)} %reshape.3.gain_ref), custom_call_target="tpu_custom_call" | custom-call | tf_op jit(solution)/shard_map/pallas_call | solution.py:164
  (9 shorter events, 0.1 us)
Async XLA Ops:
  0.0 0.8 copy-start.2
  0.8 14.1 %collective-permute-start.1 = (bf16[128,256]{1,0:T(8,128)(2,1)S(1)}, bf16[128,256]{1,0:T(8,128)(2,1)S(1)}, u32[]{:S(2)}, u32[]{:S(2)}) collective-permute-start(bf16[128,256]{1,0:T(8,128)(2,1)S(1)} %constant_dynamic-update-slice_fusion), channel_id=1, source_target_pairs={{0,32},{16,48},{32,64},{48,80},{64,96},{80,112},{96,128},{112,144}... | collective-permute-start | bytes 196616 | tf_op jit(solution)/shard_map/ppermute | solution.py:133
  6.5 11.1 %collective-permute-start = (bf16[128,256]{1,0:T(8,128)(2,1)S(1)}, bf16[128,256]{1,0:T(8,128)(2,1)S(1)}, u32[]{:S(2)}, u32[]{:S(2)}) collective-permute-start(bf16[128,256]{1,0:T(8,128)(2,1)S(1)} %constant_dynamic-update-slice_fusion), channel_id=1, source_target_pairs={{0,16},{16,32},{32,48},{48,64},{64,80},{80,96},{96,112},{112,128},... | collective-permute-start | bytes 196616 | tf_op jit(solution)/shard_map/ppermute | solution.py:133
  17.7 32.6 %collective-permute-start.2 = (bf16[384,256]{1,0:T(8,128)(2,1)S(1)}, bf16[384,256]{1,0:T(8,128)(2,1)S(1)}, u32[]{:S(2)}, u32[]{:S(2)}) collective-permute-start(bf16[384,256]{1,0:T(8,128)(2,1)S(1)} %pad_maximum_fusion.1.refs_3_), channel_id=1, source_target_pairs={{0,48},{16,64},{32,80},{48,96},{64,112},{80,128},{96,144},{112,160... | collective-permute-start | bytes 589832 | tf_op jit(solution)/shard_map/ppermute | solution.py:133
  19.6 12.4 %collective-permute-start.4 = (bf16[128,256]{1,0:T(8,128)(2,1)S(1)}, bf16[128,256]{1,0:T(8,128)(2,1)S(1)}, u32[]{:S(2)}, u32[]{:S(2)}) collective-permute-start(bf16[128,256]{1,0:T(8,128)(2,1)S(1)} %constant_dynamic-update-slice_fusion), channel_id=1, source_target_pairs={{0,160},{16,176},{32,192},{48,208},{64,224},{80,240},{96,0},{112,1... | collective-permute-start | bytes 196616 | tf_op jit(solution)/shard_map/ppermute | solution.py:133
  28.6 21.7 %collective-permute-start.3 = (bf16[128,256]{1,0:T(8,128)(2,1)S(1)}, bf16[128,256]{1,0:T(8,128)(2,1)S(1)}, u32[]{:S(2)}, u32[]{:S(2)}) collective-permute-start(bf16[128,256]{1,0:T(8,128)(2,1)S(1)} %collective-permute-done.1), channel_id=1, source_target_pairs={{0,64},{16,80},{32,96},{48,112},{64,128},{80,144},{96,160},{112,17... | collective-permute-start | bytes 196616 | tf_op jit(solution)/shard_map/ppermute | solution.py:133
  32.0 18.4 %collective-permute-start.5 = (bf16[128,256]{1,0:T(8,128)(2,1)S(1)}, bf16[128,256]{1,0:T(8,128)(2,1)S(1)}, u32[]{:S(2)}, u32[]{:S(2)}) collective-permute-start(bf16[128,256]{1,0:T(8,128)(2,1)S(1)} %collective-permute-done.4.refs_4_), channel_id=1, source_target_pairs={{0,208},{16,224},{32,240},{48,0},{64,16},{80,32},{96,48},{112,64},... | collective-permute-start | bytes 196616 | tf_op jit(solution)/shard_map/ppermute | solution.py:133
  44.4 6.0 %collective-permute-start.6 = (bf16[128,256]{1,0:T(8,128)(2,1)S(1)}, bf16[128,256]{1,0:T(8,128)(2,1)S(1)}, u32[]{:S(2)}, u32[]{:S(2)}) collective-permute-start(bf16[128,256]{1,0:T(8,128)(2,1)S(1)} %collective-permute-done.4.refs_4_), channel_id=1, source_target_pairs={{0,224},{16,240},{32,0},{48,16},{64,32},{80,48},{96,64},{112,80},{... | collective-permute-start | bytes 196616 | tf_op jit(solution)/shard_map/ppermute | solution.py:133
  48.4 5.0 %collective-permute-start.7 = (bf16[128,256]{1,0:T(8,128)(2,1)S(1)}, bf16[128,256]{1,0:T(8,128)(2,1)S(1)}, u32[]{:S(2)}, u32[]{:S(2)}) collective-permute-start(bf16[128,256]{1,0:T(8,128)(2,1)S(1)} %collective-permute-done.4.refs_4_), channel_id=1, source_target_pairs={{0,240},{16,0},{32,16},{48,32},{64,48},{80,64},{96,80},{112,96},{1... | collective-permute-start | bytes 196616 | tf_op jit(solution)/shard_map/ppermute | solution.py:133
  50.4 10.6 %copy-start = (bf16[128,1536]{1,0:T(8,128)(2,1)S(1)}, bf16[128,1536]{1,0:T(8,128)(2,1)}, u32[]{:S(2)}) copy-start(bf16[128,1536]{1,0:T(8,128)(2,1)} %refs_2_.3) | copy-start | bytes 1179652
  53.4 10.8 %collective-permute-start.8 = (bf16[896,256]{1,0:T(8,128)(2,1)S(1)}, bf16[896,256]{1,0:T(8,128)(2,1)S(1)}, u32[]{:S(2)}, u32[]{:S(2)}) collective-permute-start(bf16[896,256]{1,0:T(8,128)(2,1)S(1)} %constant_dynamic-update-slice_fusion.2), channel_id=1, source_target_pairs={{0,8},{8,0},{1,9},{9,1},{2,10},{10,2},{3,11},{11,3},{4,12},{12,4},... | collective-permute-start | bytes 1376264 | tf_op jit(solution)/shard_map/ppermute | solution.py:136
  57.5 3.4 %collective-permute-start.9 = (bf16[512,256]{1,0:T(8,128)(2,1)S(1)}, bf16[512,256]{1,0:T(8,128)(2,1)S(1)}, u32[]{:S(2)}, u32[]{:S(2)}) collective-permute-start(bf16[512,256]{1,0:T(8,128)(2,1)S(1)} %pad_maximum_fusion), channel_id=1, source_target_pairs={{0,8},{8,0},{1,9},{9,1},{2,10},{10,2},{3,11},{11,3},{4,12},{12,4},... | collective-permute-start | bytes 786440 | tf_op jit(solution)/shard_map/ppermute | solution.py:136
  59.5 1.5 %copy-start.1 = (s32[16]{0:T(128)S(1)}, s32[16]{0:T(128)}, u32[]{:S(2)}) copy-start(s32[16]{0:T(128)} %refs_1_.3) | copy-start | bytes 196
  70.0 6.8 %copy-start.3 = (bf16[1536]{0:T(1024)(128)(2,1)S(1)}, bf16[1536]{0:T(1024)(128)(2,1)}, u32[]{:S(2)}) copy-start(bf16[1536]{0:T(1024)(128)(2,1)} %param.9) | copy-start | bytes 9220
  70.0 13.4 %all-to-all-start = ((f32[8,8,128]{2,1,0:T(8,128)}), f32[8,8,128]{2,1,0:T(8,128)S(1)}, u32[]{:S(2)}, u32[]{:S(2)}) async-start(f32[8,8,128]{2,1,0:T(8,128)} %broadcast_in_dim.3), calls=%async_computation | async-start | bytes 65536 | tf_op jit(solution)/shard_map/all_to_all | solution.py:163

commit v2 on v1

v2 whole, which is shorter than its diff:
```python
import functools

import jax
import jax.numpy as jnp
from jax import lax
from jax.experimental import pallas as pl
from jax.experimental.pallas import tpu as pltpu
from jax.sharding import Mesh, PartitionSpec as P

QUERY_HEADS = 96
HEAD_SIZE = 128
ROWS = 128
MASKED = -1e30
EXP2_SCALE = HEAD_SIZE ** (-0.5) * 1.4426950408889634


def doc_starts(lengths_ref, q_pos):
    start = jnp.zeros_like(q_pos)
    end = jnp.int32(0)
    for i in range(lengths_ref.shape[0]):
        end = end + lengths_ref[i]
        start = jnp.maximum(start, jnp.where(q_pos >= end, end, 0))
    return start


def attend(layout, head_block, first, last, *refs):
    refs = list(refs)
    where_ref, lengths_ref, q_ref = refs[:3]
    pieces = refs[3 : 3 + len(layout)]
    rest = refs[3 + len(layout) :]
    if not first:
        m_in, l_in, acc_in = rest[:3]
        rest = rest[3:]
    if last:
        gain_ref, product_ref, squares_ref, bias_ref, k_ref, v_ref = rest
    else:
        m_out, l_out, acc_out, bias_ref, k_ref, v_ref = rest
    chip, core = where_ref[0], where_ref[1]
    q_pos = chip * (2 * ROWS) + core * ROWS + lax.broadcasted_iota(jnp.int32, (ROWS, ROWS), 0)
    start = doc_starts(lengths_ref, q_pos)
    lane = lax.broadcasted_iota(jnp.int32, (ROWS, ROWS), 1)
    at = 0
    for piece, blocks in zip(pieces, layout):
        for j, block in enumerate(blocks):
            if block is None:
                continue
            back, half = block
            rows = pl.ds(at * ROWS, ROWS)
            k_ref[rows, :] = piece[j * ROWS : (j + 1) * ROWS, :HEAD_SIZE]
            v_ref[rows, :HEAD_SIZE] = piece[j * ROWS : (j + 1) * ROWS, HEAD_SIZE:]
            k_pos = (chip - back) * (2 * ROWS) + half * ROWS + lane
            allowed = (k_pos >= start) & (k_pos <= q_pos)
            bias_ref[:, rows] = jnp.where(allowed, 0.0, MASKED)
            at += 1
    v_ref[:, HEAD_SIZE:] = jnp.ones_like(v_ref[:, HEAD_SIZE:])
    squares = jnp.zeros((ROWS, HEAD_SIZE), jnp.float32)
    heads = q_ref.shape[1] // HEAD_SIZE
    for h0 in range(0, heads, head_block):
        q = jnp.concatenate(
            [q_ref[:, h * HEAD_SIZE : (h + 1) * HEAD_SIZE] for h in range(h0, h0 + head_block)], axis=0
        )
        s = lax.dot_general(q, k_ref[...], (((1,), (1,)), ((), ())), preferred_element_type=jnp.float32)
        s = s.reshape(head_block, ROWS, -1) + bias_ref[...][None]
        top = jnp.max(s, axis=-1, keepdims=True)
        if not first:
            m_old = m_in[h0 : h0 + head_block]
            top = jnp.maximum(top, m_old[:, :, :1])
        p = jnp.exp2((s - top) * EXP2_SCALE).astype(jnp.bfloat16)
        out = lax.dot_general(
            p.reshape(head_block * ROWS, -1), v_ref[...], (((1,), (0,)), ((), ())), preferred_element_type=jnp.float32
        ).reshape(head_block, ROWS, 2 * HEAD_SIZE)
        acc, total = out[:, :, :HEAD_SIZE], out[:, :, HEAD_SIZE:]
        if not first:
            correct = jnp.exp2((m_old - top) * EXP2_SCALE)
            acc = acc + acc_in[h0 : h0 + head_block] * correct
            total = total + l_in[h0 : h0 + head_block] * correct
        if last:
            context = (acc / total).astype(jnp.bfloat16)
            for h in range(head_block):
                lanes = slice((h0 + h) * HEAD_SIZE, (h0 + h + 1) * HEAD_SIZE)
                wide = context[h].astype(jnp.float32)
                product_ref[:, lanes] = wide * gain_ref[:, lanes].astype(jnp.float32)
                squares = squares + wide * wide
        else:
            m_out[h0 : h0 + head_block] = jnp.broadcast_to(top, acc.shape)
            l_out[h0 : h0 + head_block] = total
            acc_out[h0 : h0 + head_block] = acc
    if last:
        summed = jnp.sum(squares.T, axis=0, keepdims=True)
        squares_ref[...] = jnp.broadcast_to(summed[None], squares_ref.shape)


def attention(where, lengths, query, pieces, layout, state, gain, head_block):
    heads = query.shape[1] // HEAD_SIZE
    keys = sum(block is not None for blocks in layout for block in blocks) * ROWS
    last = gain is not None
    vmem = pl.BlockSpec(memory_space=pltpu.VMEM)
    smem = pl.BlockSpec(memory_space=pltpu.SMEM)
    state = [] if state is None else list(state)
    tail = [gain] if last else []
    if last:
        out_shape = (
            jax.ShapeDtypeStruct(query.shape, jnp.float32),
            jax.ShapeDtypeStruct((lax.axis_size("tp"), 8, ROWS), jnp.float32),
        )
    else:
        out_shape = (jax.ShapeDtypeStruct((heads, ROWS, HEAD_SIZE), jnp.float32),) * 3
    work = heads * ROWS * keys
    return pl.pallas_call(
        functools.partial(attend, layout, head_block, not state, last),
        out_shape=out_shape,
        in_specs=[smem, smem] + [vmem] * (1 + len(pieces) + len(state) + len(tail)),
        out_specs=tuple([vmem] * len(out_shape)),
        scratch_shapes=[
            pltpu.VMEM((ROWS, keys), jnp.float32),
            pltpu.VMEM((keys, HEAD_SIZE), jnp.bfloat16),
            pltpu.VMEM((keys, 2 * HEAD_SIZE), jnp.bfloat16),
        ],
        compiler_params=pltpu.CompilerParams(vmem_limit_bytes=40 * 1024 * 1024),
        cost_estimate=pl.CostEstimate(flops=4 * work * HEAD_SIZE, bytes_accessed=4 << 20, transcendentals=work),
        name="attention_last" if last else "attention_first",
    )(where, lengths, query, *pieces, *state, *tail)


def scale_rows(product_ref, squares_ref, out_ref):
    power = jnp.sum(squares_ref[...], axis=0)[:1] / (QUERY_HEADS * HEAD_SIZE)
    factor = lax.rsqrt(jnp.broadcast_to(power, (ROWS, ROWS)).T + 1e-06)
    for h in range(product_ref.shape[1] // HEAD_SIZE):
        lanes = slice(h * HEAD_SIZE, (h + 1) * HEAD_SIZE)
        out_ref[:, lanes] = (product_ref[:, lanes] * factor).astype(jnp.bfloat16)


def halves(*distances):
    return [(back, half) for back in distances for half in (0, 1)]


def body(query, keys, values, doc_lengths, gain):
    chips = lax.axis_size("chip")
    core = lax.axis_index("core")

    def send(x, by):
        pairs = []
        for k in (0, 1):
            if by[k] is not None:
                pairs += [(z * 2 + k, (z + by[k]) % chips * 2 + k) for z in range(chips)]
        return lax.ppermute(x, ("chip", "core"), pairs)

    def share(x):
        return lax.all_gather(x, "core", axis=0, tiled=True)

    where = jnp.stack([lax.axis_index("chip"), core]).astype(jnp.int32)
    own = share(jnp.concatenate([keys, values], axis=1))
    r1_10 = send(own, (1, -6))
    r2 = send(own, (2, None))
    r345 = send(jnp.concatenate([own, r1_10, r2], axis=0), (3, None))
    r9 = send(r1_10, (None, -1))
    r87 = send(jnp.concatenate([r1_10, r9], axis=0), (None, -2))
    up = core == 0
    r6 = send(jnp.where(up, r2[:ROWS], r1_10[ROWS:]), (4, -4))
    b1_10, b2, b9 = lax.optimization_barrier((r1_10, r2, r9))
    first = share(jnp.concatenate([b1_10, jnp.where(up, b2, b9)], axis=0))
    state = attention(
        where, doc_lengths, query, (own, first),
        (halves(0), halves(1, 2, 10, 9)),
        None, None, 2,
    )
    second = share(
        jnp.where(up, jnp.concatenate([r345, r6], axis=0), jnp.concatenate([r87, r6, r345[: 2 * ROWS]], axis=0))
    )
    product, squares = attention(
        where, doc_lengths, query, (second,),
        (halves(3, 4, 5) + [(6, 0)] + halves(8, 7) + [(6, 1)] + [None] * 2,),
        state, gain.reshape(1, -1), 1,
    )
    all_squares = lax.all_to_all(squares, "tp", 0, 0)
    return pl.pallas_call(
        scale_rows,
        out_shape=jax.ShapeDtypeStruct(query.shape, jnp.bfloat16),
        compiler_params=pltpu.CompilerParams(vmem_limit_bytes=16 * 1024 * 1024),
    )(product, all_squares)


def solution(mesh):
    sizes = mesh.shape
    fine = Mesh(
        mesh.devices.reshape(sizes["dp"], sizes["ctx"] // 2, 2, sizes["tp"]), ("dp", "chip", "core", "tp")
    )
    tokens = ("dp", "chip", "core")
    return jax.shard_map(
        body,
        mesh=fine,
        in_specs=(P(tokens, "tp"), P(tokens, "tp"), P(tokens, "tp"), P("dp"), P("tp")),
        out_specs=P(tokens, "tp"),
        check_vma=False,
    )
```

time: 84.8 us -> 70 us (0.83)
  starting transfers between devices: 54.2 us -> 25.4 us
  blocking collectives: 0 us -> 26 us
  waiting for transfers between devices: 19 us -> 7.44 us
  other arithmetic: 0.11 us -> 1.08 us
    ppermute x10 -> x6, starting transfers between devices: 47.5 us -> 25.4 us  [send(): return lax.ppermute(x, ('chip', 'core'), pairs)]
    all_gather x0 -> x3, blocking collectives: none -> 13.2 us  [share(): return lax.all_gather(x, 'core', axis=0, tiled=True)]
    all_to_all x0 -> x1, blocking collectives: none -> 12.8 us  [body(): all_squares = lax.all_to_all(squares, 'tp', 0, 0)]
    all_to_all x1 -> x0, starting transfers between devices: 6.78 us -> none  [body(): lax.all_to_all(jnp.broadcast_to(squares, (8,) + squares.shape), 'tp', 0, 0)]
    all_to_all x1 -> x0, waiting for transfers between devices: 6.59 us -> none  [body(): lax.all_to_all(jnp.broadcast_to(squares, (8,) + squares.shape), 'tp', 0, 0)]
    ppermute x10 -> x6, waiting for transfers between devices: 12.4 us -> 7.44 us  [send(): return lax.ppermute(x, ('chip', 'core'), pairs)]
  transfers between devices with their start and end apart: 11 -> 6, of which waited for: 6 -> 1; matrix products, arithmetic and copies ran while one was open for 0% -> 0% of each run, Pallas kernels for 4% -> 5%
where the time goes in v2:
time: 70 us; the launch traced here: 69.6 us
  blocking collectives  26 us (37%)
  starting transfers between devices  25.4 us (36%)
  Pallas kernels  8.85 us (13%)
  waiting for transfers between devices  7.44 us (11%)
  other arithmetic  1.08 us (2%)
  local copies, waits for them, and re-layouts  0.71 us (1%)
    ppermute x6, starting transfers between devices, send(): return lax.ppermute(x, ('chip', 'core'), pairs)  25.4 us
    all_gather x3, blocking collectives, share(): return lax.all_gather(x, 'core', axis=0, tiled=True)  13.2 us
    all_to_all x1, blocking collectives, body(): all_squares = lax.all_to_all(squares, 'tp', 0, 0)  12.8 us
    pallas_call x2, Pallas kernels, attention(): pl.pallas_call(functools.partial(attend, layout, head_block, not state, l...  7.96 us
    ppermute x6, waiting for transfers between devices, send(): return lax.ppermute(x, ('chip', 'core'), pairs)  7.44 us
  transfers between devices with their start and end apart: 6, of which 1 were waited for; matrix products, arithmetic and copies ran while one was open for 0% of the time, Pallas kernels for 5%

profile of v2, /device:TPU:1, one launch (start us, length us, event | category | flops | bytes accessed | tf_op | source)
XLA Modules:
  0.0 69.6 jit_solution(14006308410052932470)
XLA Ops:
  0.0 0.8 %pad_maximum_fusion.3 = bf16[128,256]{1,0:T(8,128)(2,1)S(1)} fusion(bf16[128,128]{1,0:T(8,128)(2,1)} %param.7, bf16[128,128]{1,0:T(8,128)(2,1)} %param.6), kind=kLoop, calls=%fused_computation.6 | loop fusion | flops 131072 | bytes 131072 | tf_op jit(solution)/shard_map/concatenate | solution.py:152
  0.8 8.4 %all_gather.9.refs_3_ = bf16[256,256]{1,0:T(8,128)(2,1)S(1)} all-gather(bf16[128,256]{1,0:T(8,128)(2,1)S(1)} %pad_maximum_fusion.3), channel_id=1, replica_groups=mesh['dp'=2,'chip'=16,'core'=2,'tp'=8] {'core'}, dimensions={0}, use_global_device_ids=true | all-gather | bytes 196608 | tf_op jit(solution)/shard_map/all_gather | solution.py:149
  9.2 9.2 %collective-permute-start = (bf16[256,256]{1,0:T(8,128)(2,1)S(1)}, bf16[256,256]{1,0:T(8,128)(2,1)S(1)}, u32[]{:S(2)}, u32[]{:S(2)}) collective-permute-start(bf16[256,256]{1,0:T(8,128)(2,1)S(1)} %all_gather.9.refs_3_), channel_id=1, source_target_pairs={{0,16},{16,32},{32,48},{48,64},{64,80},{80,96},{96,112},{112,128},... | collective-permute-start | bytes 393224 | tf_op jit(solution)/shard_map/ppermute | solution.py:146
  18.4 0.7 collective-permute-start.1
  19.1 0.0 copy-start.2
  19.1 0.7 copy-done.2
  19.8 0.1 pad_add_fusion.refs_0_
  19.8 7.4 %collective-permute-done = bf16[256,256]{1,0:T(8,128)(2,1)S(1)} collective-permute-done((bf16[256,256]{1,0:T(8,128)(2,1)S(1)}, bf16[256,256]{1,0:T(8,128)(2,1)S(1)}, u32[]{:S(2)}, u32[]{:S(2)}) %collective-permute-start) | collective-permute-done | bytes 131104 | tf_op jit(solution)/shard_map/ppermute | solution.py:146
  27.3 1.9 %collective-permute-start.4 = (bf16[256,256]{1,0:T(8,128)(2,1)S(1)}, bf16[256,256]{1,0:T(8,128)(2,1)S(1)}, u32[]{:S(2)}, u32[]{:S(2)}) collective-permute-start(bf16[256,256]{1,0:T(8,128)(2,1)S(1)} %collective-permute-done), channel_id=1, source_target_pairs={{8,248},{24,8},{40,24},{56,40},{72,56},{88,72},{104,88},{120,104},... | collective-permute-start | bytes 393224 | tf_op jit(solution)/shard_map/ppermute | solution.py:146
  29.2 0.0 collective-permute-done.1
  29.2 9.7 %collective-permute-start.3 = (bf16[128,256]{1,0:T(8,128)(2,1)S(1)}, bf16[128,256]{1,0:T(8,128)(2,1)S(1)}, u32[]{:S(2)}, u32[]{:S(2)}) collective-permute-start(bf16[128,256]{1,0:T(8,128)(2,1)S(1)} %slice_select_fusion), channel_id=1, source_target_pairs={{0,64},{16,80},{32,96},{48,112},{64,128},{80,144},{96,160},{112,17... | collective-permute-start | bytes 196616 | tf_op jit(solution)/shard_map/ppermute | solution.py:146
  39.0 0.7 collective-permute-start.2
  39.7 0.0 collective-permute-done.4
  39.7 3.2 %collective-permute-start.5 = (bf16[512,256]{1,0:T(8,128)(2,1)S(1)}, bf16[512,256]{1,0:T(8,128)(2,1)S(1)}, u32[]{:S(2)}, u32[]{:S(2)}) collective-permute-start(bf16[512,256]{1,0:T(8,128)(2,1)S(1)} %pad_maximum_fusion.1), channel_id=1, source_target_pairs={{8,232},{24,248},{40,8},{56,24},{72,40},{88,56},{104,72},{120,88},... | collective-permute-start | bytes 786440 | tf_op jit(solution)/shard_map/ppermute | solution.py:146
  43.0 0.0 copy-start
  43.0 0.0 copy-start.1
  43.0 2.3 %all_gather.11.refs_4_ = bf16[1024,256]{1,0:T(8,128)(2,1)S(1)} all-gather(bf16[512,256]{1,0:T(8,128)(2,1)S(1)} %pad_maximum_fusion.2), channel_id=1, replica_groups=mesh['dp'=2,'chip'=16,'core'=2,'tp'=8] {'core'}, dimensions={0}, use_global_device_ids=true | all-gather | bytes 786432 | tf_op jit(solution)/shard_map/all_gather | solution.py:149
  45.3 0.0 copy-done
  45.3 0.0 copy-done.1
  45.3 3.7 %attention_first.1 = (f32[12,128,128]{2,1,0:T(8,128)S(1)}, f32[12,128,128]{2,1,0:T(8,128)S(1)}, f32[12,128,128]{2,1,0:T(8,128)S(1)}) custom-call(s32[2]{0:T(128)S(1)} %pad_add_fusion.refs_0_, s32[16]{0:T(128)S(1)} %copy-done.1, bf16[128,1536]{1,0:T(8,128)(2,1)S(1)} %copy-done, bf16[256,256]{1,0:T(8,128)(2,1)S(1)} %all_gather.9.refs_3_, ...), custom_call_target="tpu_custom_call" | custom-call | flops 1006632960 | bytes 4194304 | tf_op jit(solution)/shard_map/attention_first/pallas_call | solution.py:109
  49.0 0.0 collective-permute-done.2
  49.0 0.0 collective-permute-done.3
  49.0 0.0 collective-permute-done.5
  49.0 0.1 maximum_select_fusion
  49.2 2.5 %all_gather.10.refs_3_ = bf16[1792,256]{1,0:T(8,128)(2,1)S(1)} all-gather(bf16[896,256]{1,0:T(8,128)(2,1)S(1)} %maximum_select_fusion), channel_id=1, replica_groups=mesh['dp'=2,'chip'=16,'core'=2,'tp'=8] {'core'}, dimensions={0}, use_global_device_ids=true | all-gather | bytes 1376256 | tf_op jit(solution)/shard_map/all_gather | solution.py:149
  51.6 4.3 %attention_last.1 = (f32[128,1536]{1,0:T(8,128)S(1)}, f32[8,8,128]{2,1,0:T(8,128)S(1)}) custom-call(s32[2]{0:T(128)S(1)} %pad_add_fusion.refs_0_, s32[16]{0:T(128)S(1)} %copy-done.1, bf16[128,1536]{1,0:T(8,128)(2,1)S(1)} %copy-done, bf16[1792,256]{1,0:T(8,128)(2,1)S(1)} %all_gather.10.refs_3_, f32[12,128,128]{2,1,0:T(8,128)S(1)} %get-tuple-element.16.refs_4_, ...), custom_call_target="tpu_custom_call" | custom-call | flops 1207959552 | bytes 4194304 | tf_op jit(solution)/shard_map/attention_last/pallas_call | solution.py:109
  55.9 12.8 %all_to_all.5.squares_ref = f32[8,8,128]{2,1,0:T(8,128)S(1)} all-to-all(f32[8,8,128]{2,1,0:T(8,128)S(1)} %get-tuple-element.20), channel_id=1, replica_groups=mesh['dp'=2,'chip'=16,'core'=2,'tp'=8] {'tp'}, dimensions={0} | all-to-all | bytes 65536 | tf_op jit(solution)/shard_map/all_to_all | solution.py:175
  68.7 0.9 %shard_map.55 = bf16[128,1536]{1,0:T(8,128)(2,1)} custom-call(f32[128,1536]{1,0:T(8,128)S(1)} %get-tuple-element.19.product_ref, f32[8,8,128]{2,1,0:T(8,128)S(1)} %all_to_all.5.squares_ref), custom_call_target="tpu_custom_call" | custom-call | tf_op jit(solution)/shard_map/pallas_call | solution.py:176
  (7 shorter events, 0.1 us)
Async XLA Ops:
  9.2 18.1 %collective-permute-start = (bf16[256,256]{1,0:T(8,128)(2,1)S(1)}, bf16[256,256]{1,0:T(8,128)(2,1)S(1)}, u32[]{:S(2)}, u32[]{:S(2)}) collective-permute-start(bf16[256,256]{1,0:T(8,128)(2,1)S(1)} %all_gather.9.refs_3_), channel_id=1, source_target_pairs={{0,16},{16,32},{32,48},{48,64},{64,80},{80,96},{96,112},{112,128},... | collective-permute-start | bytes 393224 | tf_op jit(solution)/shard_map/ppermute | solution.py:146
  18.4 10.8 %collective-permute-start.1 = (bf16[256,256]{1,0:T(8,128)(2,1)S(1)}, bf16[256,256]{1,0:T(8,128)(2,1)S(1)}, u32[]{:S(2)}, u32[]{:S(2)}) collective-permute-start(bf16[256,256]{1,0:T(8,128)(2,1)S(1)} %all_gather.9.refs_3_), channel_id=1, source_target_pairs={{0,32},{16,48},{32,64},{48,80},{64,96},{80,112},{96,128},{112,144}... | collective-permute-start | bytes 393224 | tf_op jit(solution)/shard_map/ppermute | solution.py:146
  19.1 0.7 copy-start.2
  27.3 12.4 %collective-permute-start.4 = (bf16[256,256]{1,0:T(8,128)(2,1)S(1)}, bf16[256,256]{1,0:T(8,128)(2,1)S(1)}, u32[]{:S(2)}, u32[]{:S(2)}) collective-permute-start(bf16[256,256]{1,0:T(8,128)(2,1)S(1)} %collective-permute-done), channel_id=1, source_target_pairs={{8,248},{24,8},{40,24},{56,40},{72,56},{88,72},{104,88},{120,104},... | collective-permute-start | bytes 393224 | tf_op jit(solution)/shard_map/ppermute | solution.py:146
  29.2 19.8 %collective-permute-start.3 = (bf16[128,256]{1,0:T(8,128)(2,1)S(1)}, bf16[128,256]{1,0:T(8,128)(2,1)S(1)}, u32[]{:S(2)}, u32[]{:S(2)}) collective-permute-start(bf16[128,256]{1,0:T(8,128)(2,1)S(1)} %slice_select_fusion), channel_id=1, source_target_pairs={{0,64},{16,80},{32,96},{48,112},{64,128},{80,144},{96,160},{112,17... | collective-permute-start | bytes 196616 | tf_op jit(solution)/shard_map/ppermute | solution.py:146
  39.0 10.0 %collective-permute-start.2 = (bf16[768,256]{1,0:T(8,128)(2,1)S(1)}, bf16[768,256]{1,0:T(8,128)(2,1)S(1)}, u32[]{:S(2)}, u32[]{:S(2)}) collective-permute-start(bf16[768,256]{1,0:T(8,128)(2,1)S(1)} %pad_maximum_fusion), channel_id=1, source_target_pairs={{0,48},{16,64},{32,80},{48,96},{64,112},{80,128},{96,144},{112,160... | collective-permute-start | bytes 1179656 | tf_op jit(solution)/shard_map/ppermute | solution.py:146
  39.7 9.3 %collective-permute-start.5 = (bf16[512,256]{1,0:T(8,128)(2,1)S(1)}, bf16[512,256]{1,0:T(8,128)(2,1)S(1)}, u32[]{:S(2)}, u32[]{:S(2)}) collective-permute-start(bf16[512,256]{1,0:T(8,128)(2,1)S(1)} %pad_maximum_fusion.1), channel_id=1, source_target_pairs={{8,232},{24,248},{40,8},{56,24},{72,40},{88,56},{104,72},{120,88},... | collective-permute-start | bytes 786440 | tf_op jit(solution)/shard_map/ppermute | solution.py:146
  43.0 2.3 %copy-start = (bf16[128,1536]{1,0:T(8,128)(2,1)S(1)}, bf16[128,1536]{1,0:T(8,128)(2,1)}, u32[]{:S(2)}) copy-start(bf16[128,1536]{1,0:T(8,128)(2,1)} %refs_2_.3) | copy-start | bytes 1179652
  43.0 2.3 %copy-start.1 = (s32[16]{0:T(128)S(1)}, s32[16]{0:T(128)}, u32[]{:S(2)}) copy-start(s32[16]{0:T(128)} %refs_1_.3) | copy-start | bytes 196

commit v3 on v2

--- a/solution.py
+++ b/solution.py
@@ -138,11 +138,12 @@
     chips = lax.axis_size("chip")
     core = lax.axis_index("core")
 
-    def send(x, by):
+    def send(x, up=(), down=()):
         pairs = []
-        for k in (0, 1):
-            if by[k] is not None:
-                pairs += [(z * 2 + k, (z + by[k]) % chips * 2 + k) for z in range(chips)]
+        for k, way in enumerate((up, down)):
+            if way:
+                by, senders = way
+                pairs += [(z * 2 + k, (z + by) % chips * 2 + k) for z in senders]
         return lax.ppermute(x, ("chip", "core"), pairs)
 
     def share(x):
@@ -150,26 +151,24 @@
 
     where = jnp.stack([lax.axis_index("chip"), core]).astype(jnp.int32)
     own = share(jnp.concatenate([keys, values], axis=1))
-    r1_10 = send(own, (1, -6))
-    r2 = send(own, (2, None))
-    r345 = send(jnp.concatenate([own, r1_10, r2], axis=0), (3, None))
-    r9 = send(r1_10, (None, -1))
-    r87 = send(jnp.concatenate([r1_10, r9], axis=0), (None, -2))
+    r1_10 = send(own, up=(1, range(chips - 1)), down=(-6, range(chips - 6)))
+    r2 = send(own, up=(2, range(chips - 2)))
+    r6 = send(own, down=(6, range(chips - 6)))
+    r345 = send(jnp.concatenate([own, r1_10, r2], axis=0), up=(3, range(chips - 3)))
+    r9 = send(r1_10, down=(-1, [0, 1, 2, *range(10, chips)]))
+    r87 = send(jnp.concatenate([r1_10, r9], axis=0), down=(-2, [0, 1, *range(9, chips)]))
     up = core == 0
-    r6 = send(jnp.where(up, r2[:ROWS], r1_10[ROWS:]), (4, -4))
-    b1_10, b2, b9 = lax.optimization_barrier((r1_10, r2, r9))
-    first = share(jnp.concatenate([b1_10, jnp.where(up, b2, b9)], axis=0))
+    b1_10, b2, b9, b6 = lax.optimization_barrier((r1_10, r2, r9, r6))
+    first = share(jnp.concatenate([b1_10, jnp.where(up, b2, b9), b6], axis=0))
     state = attention(
         where, doc_lengths, query, (own, first),
-        (halves(0), halves(1, 2, 10, 9)),
+        (halves(0), halves(1, 2) + [None, None] + halves(10, 9, 6)),
         None, None, 2,
     )
-    second = share(
-        jnp.where(up, jnp.concatenate([r345, r6], axis=0), jnp.concatenate([r87, r6, r345[: 2 * ROWS]], axis=0))
-    )
+    second = share(jnp.where(up, r345, jnp.concatenate([r87, r345[: 2 * ROWS]], axis=0)))
     product, squares = attention(
         where, doc_lengths, query, (second,),
-        (halves(3, 4, 5) + [(6, 0)] + halves(8, 7) + [(6, 1)] + [None] * 2,),
+        (halves(3, 4, 5, 8, 7) + [None, None],),
         state, gain.reshape(1, -1), 1,
     )
     all_squares = lax.all_to_all(squares, "tp", 0, 0)

time: 70 us -> 67.7 us (0.967)
  the two profiles are of different devices: /device:TPU:1 before, /device:TPU:160 now
where the time goes in v3:
time: 67.7 us; the launch traced here: 67.4 us
  blocking collectives  21.2 us (31%)
  starting transfers between devices  20.1 us (30%)
  waiting for transfers between devices  15.6 us (23%)
  Pallas kernels  9.25 us (14%)
  other arithmetic  1.06 us (2%)
    ppermute x6, starting transfers between devices, send(): return lax.ppermute(x, ('chip', 'core'), pairs)  20.1 us
    ppermute x6, waiting for transfers between devices, send(): return lax.ppermute(x, ('chip', 'core'), pairs)  15.6 us
    all_to_all x1, blocking collectives, body(): all_squares = lax.all_to_all(squares, 'tp', 0, 0)  14.4 us
    pallas_call x2, Pallas kernels, attention(): pl.pallas_call(functools.partial(attend, layout, head_block, not state, l...  8.36 us
    all_gather x3, blocking collectives, share(): return lax.all_gather(x, 'core', axis=0, tiled=True)  6.76 us
  transfers between devices with their start and end apart: 6, of which 2 were waited for; matrix products, arithmetic and copies ran while one was open for 0% of the time, Pallas kernels for 6%

profile of v3, /device:TPU:160, one launch (start us, length us, event | category | flops | bytes accessed | tf_op | source)
XLA Modules:
  0.0 67.4 jit_solution(1081845783052304561)
XLA Ops:
  0.0 0.8 %pad_maximum_fusion.3 = bf16[128,256]{1,0:T(8,128)(2,1)S(1)} fusion(bf16[128,128]{1,0:T(8,128)(2,1)} %param.7, bf16[128,128]{1,0:T(8,128)(2,1)} %param.6), kind=kLoop, calls=%fused_computation.5 | loop fusion | flops 131072 | bytes 131072 | tf_op jit(solution)/shard_map/concatenate | solution.py:153
  0.8 1.9 %all_gather.9.refs_3_ = bf16[256,256]{1,0:T(8,128)(2,1)S(1)} all-gather(bf16[128,256]{1,0:T(8,128)(2,1)S(1)} %pad_maximum_fusion.3), channel_id=1, replica_groups=mesh['dp'=2,'chip'=16,'core'=2,'tp'=8] {'core'}, dimensions={0}, use_global_device_ids=true | all-gather | bytes 196608 | tf_op jit(solution)/shard_map/all_gather | solution.py:150
  2.7 3.8 %collective-permute-start = (bf16[256,256]{1,0:T(8,128)(2,1)S(1)}, bf16[256,256]{1,0:T(8,128)(2,1)S(1)}, u32[]{:S(2)}, u32[]{:S(2)}) collective-permute-start(bf16[256,256]{1,0:T(8,128)(2,1)S(1)} %all_gather.9.refs_3_), channel_id=1, source_target_pairs={{0,16},{16,32},{32,48},{48,64},{64,80},{80,96},{96,112},{112,128},... | collective-permute-start | bytes 393224 | tf_op jit(solution)/shard_map/ppermute | solution.py:147
  6.5 6.4 %collective-permute-start.1 = (bf16[256,256]{1,0:T(8,128)(2,1)S(1)}, bf16[256,256]{1,0:T(8,128)(2,1)S(1)}, u32[]{:S(2)}, u32[]{:S(2)}) collective-permute-start(bf16[256,256]{1,0:T(8,128)(2,1)S(1)} %all_gather.9.refs_3_), channel_id=1, source_target_pairs={{0,32},{16,48},{32,64},{48,80},{64,96},{80,112},{96,128},{112,144}... | collective-permute-start | bytes 393224 | tf_op jit(solution)/shard_map/ppermute | solution.py:147
  12.9 0.7 collective-permute-start.5
  13.6 0.0 copy-start.2
  13.6 0.0 collective-permute-done
  13.6 0.7 collective-permute-start.3
  14.3 0.1 pad_add_fusion.refs_0_
  14.4 0.0 copy-done.2
  14.4 9.9 %collective-permute-done.1 = bf16[256,256]{1,0:T(8,128)(2,1)S(1)} collective-permute-done((bf16[256,256]{1,0:T(8,128)(2,1)S(1)}, bf16[256,256]{1,0:T(8,128)(2,1)S(1)}, u32[]{:S(2)}, u32[]{:S(2)}) %collective-permute-start.1) | collective-permute-done | bytes 131104 | tf_op jit(solution)/shard_map/ppermute | solution.py:147
  24.3 7.9 %collective-permute-start.2 = (bf16[768,256]{1,0:T(8,128)(2,1)S(1)}, bf16[768,256]{1,0:T(8,128)(2,1)S(1)}, u32[]{:S(2)}, u32[]{:S(2)}) collective-permute-start(bf16[768,256]{1,0:T(8,128)(2,1)S(1)} %pad_maximum_fusion), channel_id=1, source_target_pairs={{0,48},{16,64},{32,80},{48,96},{64,112},{80,128},{96,144},{112,160... | collective-permute-start | bytes 1179656 | tf_op jit(solution)/shard_map/ppermute | solution.py:147
  32.2 0.0 collective-permute-done.5
  32.2 0.0 collective-permute-done.3
  32.2 0.7 %collective-permute-start.4 = (bf16[512,256]{1,0:T(8,128)(2,1)S(1)}, bf16[512,256]{1,0:T(8,128)(2,1)S(1)}, u32[]{:S(2)}, u32[]{:S(2)}) collective-permute-start(bf16[512,256]{1,0:T(8,128)(2,1)S(1)} %pad_maximum_fusion.2), channel_id=1, source_target_pairs={{8,232},{24,248},{152,120},{168,136},{184,152},{200,168},{216,184}... | collective-permute-start | bytes 786440 | tf_op jit(solution)/shard_map/ppermute | solution.py:147
  33.0 0.0 copy-start
  33.0 0.0 copy-start.1
  33.0 2.5 %all_gather.11.refs_4_ = bf16[1536,256]{1,0:T(8,128)(2,1)S(1)} all-gather(bf16[768,256]{1,0:T(8,128)(2,1)S(1)} %pad_maximum_fusion.1), channel_id=1, replica_groups=mesh['dp'=2,'chip'=16,'core'=2,'tp'=8] {'core'}, dimensions={0}, use_global_device_ids=true | all-gather | bytes 1179648 | tf_op jit(solution)/shard_map/all_gather | solution.py:150
  35.5 0.0 copy-done
  35.5 0.0 copy-done.1
  35.5 4.4 %attention_first.1 = (f32[12,128,128]{2,1,0:T(8,128)S(1)}, f32[12,128,128]{2,1,0:T(8,128)S(1)}, f32[12,128,128]{2,1,0:T(8,128)S(1)}) custom-call(s32[2]{0:T(128)S(1)} %pad_add_fusion.refs_0_, s32[16]{0:T(128)S(1)} %copy-done.1, bf16[128,1536]{1,0:T(8,128)(2,1)S(1)} %copy-done, bf16[256,256]{1,0:T(8,128)(2,1)S(1)} %all_gather.9.refs_3_, ...), custom_call_target="tpu_custom_call" | custom-call | flops 1207959552 | bytes 4194304 | tf_op jit(solution)/shard_map/attention_first/pallas_call | solution.py:109
  39.9 5.7 %collective-permute-done.2 = bf16[768,256]{1,0:T(8,128)(2,1)S(1)} collective-permute-done((bf16[768,256]{1,0:T(8,128)(2,1)S(1)}, bf16[768,256]{1,0:T(8,128)(2,1)S(1)}, u32[]{:S(2)}, u32[]{:S(2)}) %collective-permute-start.2) | collective-permute-done | bytes 393248 | tf_op jit(solution)/shard_map/ppermute | solution.py:147
  45.6 0.0 collective-permute-done.4
  45.6 0.1 maximum_select_fusion
  45.7 2.4 %all_gather.10.refs_3_ = bf16[1536,256]{1,0:T(8,128)(2,1)S(1)} all-gather(bf16[768,256]{1,0:T(8,128)(2,1)S(1)} %maximum_select_fusion), channel_id=1, replica_groups=mesh['dp'=2,'chip'=16,'core'=2,'tp'=8] {'core'}, dimensions={0}, use_global_device_ids=true | all-gather | bytes 1179648 | tf_op jit(solution)/shard_map/all_gather | solution.py:150
  48.1 4.0 %attention_last.1 = (f32[128,1536]{1,0:T(8,128)S(1)}, f32[8,8,128]{2,1,0:T(8,128)S(1)}) custom-call(s32[2]{0:T(128)S(1)} %pad_add_fusion.refs_0_, s32[16]{0:T(128)S(1)} %copy-done.1, bf16[128,1536]{1,0:T(8,128)(2,1)S(1)} %copy-done, bf16[1536,256]{1,0:T(8,128)(2,1)S(1)} %all_gather.10.refs_3_, f32[12,128,128]{2,1,0:T(8,128)S(1)} %get-tuple-element.18.refs_4_, ...), custom_call_target="tpu_custom_call" | custom-call | flops 1006632960 | bytes 4194304 | tf_op jit(solution)/shard_map/attention_last/pallas_call | solution.py:109
  52.1 14.4 %all_to_all.5.squares_ref = f32[8,8,128]{2,1,0:T(8,128)S(1)} all-to-all(f32[8,8,128]{2,1,0:T(8,128)S(1)} %get-tuple-element.22), channel_id=1, replica_groups=mesh['dp'=2,'chip'=16,'core'=2,'tp'=8] {'tp'}, dimensions={0} | all-to-all | bytes 65536 | tf_op jit(solution)/shard_map/all_to_all | solution.py:174
  66.5 0.9 %shard_map.55 = bf16[128,1536]{1,0:T(8,128)(2,1)} custom-call(f32[128,1536]{1,0:T(8,128)S(1)} %get-tuple-element.21.product_ref, f32[8,8,128]{2,1,0:T(8,128)S(1)} %all_to_all.5.squares_ref), custom_call_target="tpu_custom_call" | custom-call | tf_op jit(solution)/shard_map/pallas_call | solution.py:175
  (6 shorter events, 0.1 us)
Async XLA Ops:
  2.7 10.9 %collective-permute-start = (bf16[256,256]{1,0:T(8,128)(2,1)S(1)}, bf16[256,256]{1,0:T(8,128)(2,1)S(1)}, u32[]{:S(2)}, u32[]{:S(2)}) collective-permute-start(bf16[256,256]{1,0:T(8,128)(2,1)S(1)} %all_gather.9.refs_3_), channel_id=1, source_target_pairs={{0,16},{16,32},{32,48},{48,64},{64,80},{80,96},{96,112},{112,128},... | collective-permute-start | bytes 393224 | tf_op jit(solution)/shard_map/ppermute | solution.py:147
  6.5 17.8 %collective-permute-start.1 = (bf16[256,256]{1,0:T(8,128)(2,1)S(1)}, bf16[256,256]{1,0:T(8,128)(2,1)S(1)}, u32[]{:S(2)}, u32[]{:S(2)}) collective-permute-start(bf16[256,256]{1,0:T(8,128)(2,1)S(1)} %all_gather.9.refs_3_), channel_id=1, source_target_pairs={{0,32},{16,48},{32,64},{48,80},{64,96},{80,112},{96,128},{112,144}... | collective-permute-start | bytes 393224 | tf_op jit(solution)/shard_map/ppermute | solution.py:147
  12.9 19.3 %collective-permute-start.5 = (bf16[256,256]{1,0:T(8,128)(2,1)S(1)}, bf16[256,256]{1,0:T(8,128)(2,1)S(1)}, u32[]{:S(2)}, u32[]{:S(2)}) collective-permute-start(bf16[256,256]{1,0:T(8,128)(2,1)S(1)} %all_gather.9.refs_3_), channel_id=1, source_target_pairs={{8,104},{24,120},{40,136},{56,152},{72,168},{88,184},{104,200},{12... | collective-permute-start | bytes 393224 | tf_op jit(solution)/shard_map/ppermute | solution.py:147
  13.6 0.8 %copy-start.2 = (bf16[1536]{0:T(1024)(128)(2,1)S(1)}, bf16[1536]{0:T(1024)(128)(2,1)}, u32[]{:S(2)}) copy-start(bf16[1536]{0:T(1024)(128)(2,1)} %param.9) | copy-start | bytes 9220
  13.6 18.6 %collective-permute-start.3 = (bf16[256,256]{1,0:T(8,128)(2,1)S(1)}, bf16[256,256]{1,0:T(8,128)(2,1)S(1)}, u32[]{:S(2)}, u32[]{:S(2)}) collective-permute-start(bf16[256,256]{1,0:T(8,128)(2,1)S(1)} %collective-permute-done), channel_id=1, source_target_pairs={{8,248},{24,8},{40,24},{168,152},{184,168},{200,184},{216,200},{23... | collective-permute-start | bytes 393224 | tf_op jit(solution)/shard_map/ppermute | solution.py:147
  24.3 21.3 %collective-permute-start.2 = (bf16[768,256]{1,0:T(8,128)(2,1)S(1)}, bf16[768,256]{1,0:T(8,128)(2,1)S(1)}, u32[]{:S(2)}, u32[]{:S(2)}) collective-permute-start(bf16[768,256]{1,0:T(8,128)(2,1)S(1)} %pad_maximum_fusion), channel_id=1, source_target_pairs={{0,48},{16,64},{32,80},{48,96},{64,112},{80,128},{96,144},{112,160... | collective-permute-start | bytes 1179656 | tf_op jit(solution)/shard_map/ppermute | solution.py:147
  32.2 13.4 %collective-permute-start.4 = (bf16[512,256]{1,0:T(8,128)(2,1)S(1)}, bf16[512,256]{1,0:T(8,128)(2,1)S(1)}, u32[]{:S(2)}, u32[]{:S(2)}) collective-permute-start(bf16[512,256]{1,0:T(8,128)(2,1)S(1)} %pad_maximum_fusion.2), channel_id=1, source_target_pairs={{8,232},{24,248},{152,120},{168,136},{184,152},{200,168},{216,184}... | collective-permute-start | bytes 786440 | tf_op jit(solution)/shard_map/ppermute | solution.py:147
  33.0 2.5 %copy-start = (bf16[128,1536]{1,0:T(8,128)(2,1)S(1)}, bf16[128,1536]{1,0:T(8,128)(2,1)}, u32[]{:S(2)}) copy-start(bf16[128,1536]{1,0:T(8,128)(2,1)} %refs_2_.3) | copy-start | bytes 1179652
  33.0 2.5 %copy-start.1 = (s32[16]{0:T(128)S(1)}, s32[16]{0:T(128)}, u32[]{:S(2)}) copy-start(s32[16]{0:T(128)} %refs_1_.3) | copy-start | bytes 196

commit v4 on v3

--- a/solution.py
+++ b/solution.py
@@ -153,22 +153,23 @@
     own = share(jnp.concatenate([keys, values], axis=1))
     r1_10 = send(own, up=(1, range(chips - 1)), down=(-6, range(chips - 6)))
     r2 = send(own, up=(2, range(chips - 2)))
-    r6 = send(own, down=(6, range(chips - 6)))
+    late, _ = lax.optimization_barrier((own, r1_10))
+    r6 = send(late, down=(6, range(chips - 6)))
     r345 = send(jnp.concatenate([own, r1_10, r2], axis=0), up=(3, range(chips - 3)))
     r9 = send(r1_10, down=(-1, [0, 1, 2, *range(10, chips)]))
     r87 = send(jnp.concatenate([r1_10, r9], axis=0), down=(-2, [0, 1, *range(9, chips)]))
     up = core == 0
-    b1_10, b2, b9, b6 = lax.optimization_barrier((r1_10, r2, r9, r6))
-    first = share(jnp.concatenate([b1_10, jnp.where(up, b2, b9), b6], axis=0))
+    b1_10, b2, b9 = lax.optimization_barrier((r1_10, r2, r9))
+    first = share(jnp.concatenate([b1_10, jnp.where(up, b2, b9)], axis=0))
     state = attention(
         where, doc_lengths, query, (own, first),
-        (halves(0), halves(1, 2) + [None, None] + halves(10, 9, 6)),
+        (halves(0), halves(1, 2, 10, 9)),
         None, None, 2,
     )
-    second = share(jnp.where(up, r345, jnp.concatenate([r87, r345[: 2 * ROWS]], axis=0)))
+    second = share(jnp.where(up, r345, jnp.concatenate([r87, r6], axis=0)))
     product, squares = attention(
         where, doc_lengths, query, (second,),
-        (halves(3, 4, 5, 8, 7) + [None, None],),
+        (halves(3, 4, 5, 8, 7, 6),),
         state, gain.reshape(1, -1), 1,
     )
     all_squares = lax.all_to_all(squares, "tp", 0, 0)

time: 67.7 us -> 65.4 us (0.966)
  waiting for transfers between devices: 15.6 us -> 4.22 us
  blocking collectives: 21.2 us -> 31.7 us
  starting transfers between devices: 20.1 us -> 19.1 us
    ppermute x6, waiting for transfers between devices: 15.6 us -> 4.22 us  [send(): return lax.ppermute(x, ('chip', 'core'), pairs)]
    all_gather x3, blocking collectives: 6.76 us -> 17.2 us  [share(): return lax.all_gather(x, 'core', axis=0, tiled=True)]
    ppermute x6, starting transfers between devices: 20.1 us -> 19.1 us  [send(): return lax.ppermute(x, ('chip', 'core'), pairs)]
where the time goes in v4:
time: 65.4 us; the launch traced here: 65.1 us
  blocking collectives  31.7 us (48%)
  starting transfers between devices  19.1 us (29%)
  Pallas kernels  8.82 us (13%)
  waiting for transfers between devices  4.22 us (6%)
  other arithmetic  1.05 us (2%)
    ppermute x6, starting transfers between devices, send(): return lax.ppermute(x, ('chip', 'core'), pairs)  19.1 us
    all_gather x3, blocking collectives, share(): return lax.all_gather(x, 'core', axis=0, tiled=True)  17.2 us
    all_to_all x1, blocking collectives, body(): all_squares = lax.all_to_all(squares, 'tp', 0, 0)  14.5 us
    pallas_call x2, Pallas kernels, attention(): pl.pallas_call(functools.partial(attend, layout, head_block, not state, l...  7.93 us
    ppermute x6, waiting for transfers between devices, send(): return lax.ppermute(x, ('chip', 'core'), pairs)  4.22 us
  transfers between devices with their start and end apart: 6, of which 2 were waited for; matrix products, arithmetic and copies ran while one was open for 0% of the time, Pallas kernels for 6%

profile of v4, /device:TPU:160, one launch (start us, length us, event | category | flops | bytes accessed | tf_op | source)
XLA Modules:
  0.0 65.1 jit_solution(6905718715214026501)
XLA Ops:
  0.0 0.8 %pad_maximum_fusion.3 = bf16[128,256]{1,0:T(8,128)(2,1)S(1)} fusion(bf16[128,128]{1,0:T(8,128)(2,1)} %param.7, bf16[128,128]{1,0:T(8,128)(2,1)} %param.6), kind=kLoop, calls=%fused_computation.5 | loop fusion | flops 131072 | bytes 131072 | tf_op jit(solution)/shard_map/concatenate | solution.py:153
  0.8 1.9 %all_gather.9.refs_3_ = bf16[256,256]{1,0:T(8,128)(2,1)S(1)} all-gather(bf16[128,256]{1,0:T(8,128)(2,1)S(1)} %pad_maximum_fusion.3), channel_id=1, replica_groups=mesh['dp'=2,'chip'=16,'core'=2,'tp'=8] {'core'}, dimensions={0}, use_global_device_ids=true | all-gather | bytes 196608 | tf_op jit(solution)/shard_map/all_gather | solution.py:150
  2.7 3.8 %collective-permute-start = (bf16[256,256]{1,0:T(8,128)(2,1)S(1)}, bf16[256,256]{1,0:T(8,128)(2,1)S(1)}, u32[]{:S(2)}, u32[]{:S(2)}) collective-permute-start(bf16[256,256]{1,0:T(8,128)(2,1)S(1)} %all_gather.9.refs_3_), channel_id=1, source_target_pairs={{0,16},{16,32},{32,48},{48,64},{64,80},{80,96},{96,112},{112,128},... | collective-permute-start | bytes 393224 | tf_op jit(solution)/shard_map/ppermute | solution.py:147
  6.5 6.4 %collective-permute-start.1 = (bf16[256,256]{1,0:T(8,128)(2,1)S(1)}, bf16[256,256]{1,0:T(8,128)(2,1)S(1)}, u32[]{:S(2)}, u32[]{:S(2)}) collective-permute-start(bf16[256,256]{1,0:T(8,128)(2,1)S(1)} %all_gather.9.refs_3_), channel_id=1, source_target_pairs={{0,32},{16,48},{32,64},{48,80},{64,96},{80,112},{96,128},{112,144}... | collective-permute-start | bytes 393224 | tf_op jit(solution)/shard_map/ppermute | solution.py:147
  12.9 0.0 copy-start.2
  12.9 0.0 collective-permute-done
  12.9 0.7 %collective-permute-start.3 = (bf16[256,256]{1,0:T(8,128)(2,1)S(1)}, bf16[256,256]{1,0:T(8,128)(2,1)S(1)}, u32[]{:S(2)}, u32[]{:S(2)}) collective-permute-start(bf16[256,256]{1,0:T(8,128)(2,1)S(1)} %collective-permute-done), channel_id=1, source_target_pairs={{8,248},{24,8},{40,24},{168,152},{184,168},{200,184},{216,200},{23... | collective-permute-start | bytes 393224 | tf_op jit(solution)/shard_map/ppermute | solution.py:147
  13.6 0.1 pad_add_fusion.refs_0_
  13.7 0.0 copy-done.2
  13.7 0.7 %collective-permute-start.5 = (bf16[256,256]{1,0:T(8,128)(2,1)S(1)}, bf16[256,256]{1,0:T(8,128)(2,1)S(1)}, u32[]{:S(2)}, u32[]{:S(2)}) collective-permute-start(bf16[256,256]{1,0:T(8,128)(2,1)S(1)} %all_gather.9.refs_3_), channel_id=1, source_target_pairs={{8,104},{24,120},{40,136},{56,152},{72,168},{88,184},{104,200},{12... | collective-permute-start | bytes 393224 | tf_op jit(solution)/shard_map/ppermute | solution.py:147
  14.4 2.5 %collective-permute-done.1 = bf16[256,256]{1,0:T(8,128)(2,1)S(1)} collective-permute-done((bf16[256,256]{1,0:T(8,128)(2,1)S(1)}, bf16[256,256]{1,0:T(8,128)(2,1)S(1)}, u32[]{:S(2)}, u32[]{:S(2)}) %collective-permute-start.1) | collective-permute-done | bytes 131104 | tf_op jit(solution)/shard_map/ppermute | solution.py:147
  16.9 6.9 %collective-permute-start.2 = (bf16[768,256]{1,0:T(8,128)(2,1)S(1)}, bf16[768,256]{1,0:T(8,128)(2,1)S(1)}, u32[]{:S(2)}, u32[]{:S(2)}) collective-permute-start(bf16[768,256]{1,0:T(8,128)(2,1)S(1)} %pad_maximum_fusion), channel_id=1, source_target_pairs={{0,48},{16,64},{32,80},{48,96},{64,112},{80,128},{96,144},{112,160... | collective-permute-start | bytes 1179656 | tf_op jit(solution)/shard_map/ppermute | solution.py:147
  23.8 0.0 collective-permute-done.3
  23.8 0.7 %collective-permute-start.4 = (bf16[512,256]{1,0:T(8,128)(2,1)S(1)}, bf16[512,256]{1,0:T(8,128)(2,1)S(1)}, u32[]{:S(2)}, u32[]{:S(2)}) collective-permute-start(bf16[512,256]{1,0:T(8,128)(2,1)S(1)} %pad_maximum_fusion.1), channel_id=1, source_target_pairs={{8,232},{24,248},{152,120},{168,136},{184,152},{200,168},{216,184}... | collective-permute-start | bytes 786440 | tf_op jit(solution)/shard_map/ppermute | solution.py:147
  24.5 0.0 copy-start
  24.5 0.0 copy-start.1
  24.6 12.9 %all_gather.11.refs_4_ = bf16[1024,256]{1,0:T(8,128)(2,1)S(1)} all-gather(bf16[512,256]{1,0:T(8,128)(2,1)S(1)} %pad_maximum_fusion.2), channel_id=1, replica_groups=mesh['dp'=2,'chip'=16,'core'=2,'tp'=8] {'core'}, dimensions={0}, use_global_device_ids=true | all-gather | bytes 786432 | tf_op jit(solution)/shard_map/all_gather | solution.py:150
  37.5 0.0 copy-done
  37.5 0.0 copy-done.1
  37.5 3.7 %attention_first.1 = (f32[12,128,128]{2,1,0:T(8,128)S(1)}, f32[12,128,128]{2,1,0:T(8,128)S(1)}, f32[12,128,128]{2,1,0:T(8,128)S(1)}) custom-call(s32[2]{0:T(128)S(1)} %pad_add_fusion.refs_0_, s32[16]{0:T(128)S(1)} %copy-done.1, bf16[128,1536]{1,0:T(8,128)(2,1)S(1)} %copy-done, bf16[256,256]{1,0:T(8,128)(2,1)S(1)} %all_gather.9.refs_3_, ...), custom_call_target="tpu_custom_call" | custom-call | flops 1006632960 | bytes 4194304 | tf_op jit(solution)/shard_map/attention_first/pallas_call | solution.py:109
  41.2 0.0 collective-permute-done.5
  41.2 0.0 collective-permute-done.4
  41.2 1.7 %collective-permute-done.2 = bf16[768,256]{1,0:T(8,128)(2,1)S(1)} collective-permute-done((bf16[768,256]{1,0:T(8,128)(2,1)S(1)}, bf16[768,256]{1,0:T(8,128)(2,1)S(1)}, u32[]{:S(2)}, u32[]{:S(2)}) %collective-permute-start.2) | collective-permute-done | bytes 393248 | tf_op jit(solution)/shard_map/ppermute | solution.py:147
  42.9 0.1 maximum_select_fusion
  43.0 2.4 %all_gather.10.refs_3_ = bf16[1536,256]{1,0:T(8,128)(2,1)S(1)} all-gather(bf16[768,256]{1,0:T(8,128)(2,1)S(1)} %maximum_select_fusion), channel_id=1, replica_groups=mesh['dp'=2,'chip'=16,'core'=2,'tp'=8] {'core'}, dimensions={0}, use_global_device_ids=true | all-gather | bytes 1179648 | tf_op jit(solution)/shard_map/all_gather | solution.py:150
  45.4 4.3 %attention_last.1 = (f32[128,1536]{1,0:T(8,128)S(1)}, f32[8,8,128]{2,1,0:T(8,128)S(1)}) custom-call(s32[2]{0:T(128)S(1)} %pad_add_fusion.refs_0_, s32[16]{0:T(128)S(1)} %copy-done.1, bf16[128,1536]{1,0:T(8,128)(2,1)S(1)} %copy-done, bf16[1536,256]{1,0:T(8,128)(2,1)S(1)} %all_gather.10.refs_3_, f32[12,128,128]{2,1,0:T(8,128)S(1)} %get-tuple-element.18.refs_4_, ...), custom_call_target="tpu_custom_call" | custom-call | flops 1207959552 | bytes 4194304 | tf_op jit(solution)/shard_map/attention_last/pallas_call | solution.py:109
  49.7 14.5 %all_to_all.5.squares_ref = f32[8,8,128]{2,1,0:T(8,128)S(1)} all-to-all(f32[8,8,128]{2,1,0:T(8,128)S(1)} %get-tuple-element.22), channel_id=1, replica_groups=mesh['dp'=2,'chip'=16,'core'=2,'tp'=8] {'tp'}, dimensions={0} | all-to-all | bytes 65536 | tf_op jit(solution)/shard_map/all_to_all | solution.py:175
  64.2 0.9 %shard_map.55 = bf16[128,1536]{1,0:T(8,128)(2,1)} custom-call(f32[128,1536]{1,0:T(8,128)S(1)} %get-tuple-element.21.product_ref, f32[8,8,128]{2,1,0:T(8,128)S(1)} %all_to_all.5.squares_ref), custom_call_target="tpu_custom_call" | custom-call | tf_op jit(solution)/shard_map/pallas_call | solution.py:176
  (5 shorter events, 0.1 us)
Async XLA Ops:
  2.7 10.2 %collective-permute-start = (bf16[256,256]{1,0:T(8,128)(2,1)S(1)}, bf16[256,256]{1,0:T(8,128)(2,1)S(1)}, u32[]{:S(2)}, u32[]{:S(2)}) collective-permute-start(bf16[256,256]{1,0:T(8,128)(2,1)S(1)} %all_gather.9.refs_3_), channel_id=1, source_target_pairs={{0,16},{16,32},{32,48},{48,64},{64,80},{80,96},{96,112},{112,128},... | collective-permute-start | bytes 393224 | tf_op jit(solution)/shard_map/ppermute | solution.py:147
  6.5 10.3 %collective-permute-start.1 = (bf16[256,256]{1,0:T(8,128)(2,1)S(1)}, bf16[256,256]{1,0:T(8,128)(2,1)S(1)}, u32[]{:S(2)}, u32[]{:S(2)}) collective-permute-start(bf16[256,256]{1,0:T(8,128)(2,1)S(1)} %all_gather.9.refs_3_), channel_id=1, source_target_pairs={{0,32},{16,48},{32,64},{48,80},{64,96},{80,112},{96,128},{112,144}... | collective-permute-start | bytes 393224 | tf_op jit(solution)/shard_map/ppermute | solution.py:147
  12.9 0.8 %copy-start.2 = (bf16[1536]{0:T(1024)(128)(2,1)S(1)}, bf16[1536]{0:T(1024)(128)(2,1)}, u32[]{:S(2)}) copy-start(bf16[1536]{0:T(1024)(128)(2,1)} %param.9) | copy-start | bytes 9220
  12.9 10.8 %collective-permute-start.3 = (bf16[256,256]{1,0:T(8,128)(2,1)S(1)}, bf16[256,256]{1,0:T(8,128)(2,1)S(1)}, u32[]{:S(2)}, u32[]{:S(2)}) collective-permute-start(bf16[256,256]{1,0:T(8,128)(2,1)S(1)} %collective-permute-done), channel_id=1, source_target_pairs={{8,248},{24,8},{40,24},{168,152},{184,168},{200,184},{216,200},{23... | collective-permute-start | bytes 393224 | tf_op jit(solution)/shard_map/ppermute | solution.py:147
  13.7 27.5 %collective-permute-start.5 = (bf16[256,256]{1,0:T(8,128)(2,1)S(1)}, bf16[256,256]{1,0:T(8,128)(2,1)S(1)}, u32[]{:S(2)}, u32[]{:S(2)}) collective-permute-start(bf16[256,256]{1,0:T(8,128)(2,1)S(1)} %all_gather.9.refs_3_), channel_id=1, source_target_pairs={{8,104},{24,120},{40,136},{56,152},{72,168},{88,184},{104,200},{12... | collective-permute-start | bytes 393224 | tf_op jit(solution)/shard_map/ppermute | solution.py:147
  16.9 26.1 %collective-permute-start.2 = (bf16[768,256]{1,0:T(8,128)(2,1)S(1)}, bf16[768,256]{1,0:T(8,128)(2,1)S(1)}, u32[]{:S(2)}, u32[]{:S(2)}) collective-permute-start(bf16[768,256]{1,0:T(8,128)(2,1)S(1)} %pad_maximum_fusion), channel_id=1, source_target_pairs={{0,48},{16,64},{32,80},{48,96},{64,112},{80,128},{96,144},{112,160... | collective-permute-start | bytes 1179656 | tf_op jit(solution)/shard_map/ppermute | solution.py:147
  23.8 17.4 %collective-permute-start.4 = (bf16[512,256]{1,0:T(8,128)(2,1)S(1)}, bf16[512,256]{1,0:T(8,128)(2,1)S(1)}, u32[]{:S(2)}, u32[]{:S(2)}) collective-permute-start(bf16[512,256]{1,0:T(8,128)(2,1)S(1)} %pad_maximum_fusion.1), channel_id=1, source_target_pairs={{8,232},{24,248},{152,120},{168,136},{184,152},{200,168},{216,184}... | collective-permute-start | bytes 786440 | tf_op jit(solution)/shard_map/ppermute | solution.py:147
  24.5 13.0 %copy-start = (bf16[128,1536]{1,0:T(8,128)(2,1)S(1)}, bf16[128,1536]{1,0:T(8,128)(2,1)}, u32[]{:S(2)}) copy-start(bf16[128,1536]{1,0:T(8,128)(2,1)} %refs_2_.3) | copy-start | bytes 1179652
  24.5 12.9 %copy-start.1 = (s32[16]{0:T(128)S(1)}, s32[16]{0:T(128)}, u32[]{:S(2)}) copy-start(s32[16]{0:T(128)} %refs_1_.3) | copy-start | bytes 196
